TPU v7x, 32 devices: a whole 2x2x4 slice. The times are simulated.
32 devices in a mesh: ctx: 16 (over z, y, core), fsdp: 2 (over x).
Axes of the slice: x: 2, y: 2, z: 4, core: 2. Of those that a mesh axis runs over, the one named last changes fastest.
Arguments:
- tokens_in: bfloat16 [4, 2048, 1024], P('fsdp', 'ctx'), may hold values from -6 to 6
- gain_attn: bfloat16 [1024], P('fsdp'), may hold values from 0.5 to 1.5
- shift_attn: bfloat16 [1024], P('fsdp'), may hold values from -4 to 4
- w_heads: bfloat16 [1024, 3072], P('fsdp'), may hold values from -0.1875 to 0.1875
- bias_query: bfloat16 [1024], P('fsdp'), may hold values from -4 to 4
- bias_value: bfloat16 [1024], P('fsdp'), may hold values from -0.75 to 0.75
- w_merge: bfloat16 [1024, 1024], P('fsdp'), may hold values from -0.75 to 0.75
- bias_merge: bfloat16 [1024], P('fsdp'), may hold values from -4 to 4
- gain_mlp: bfloat16 [1024], P('fsdp'), may hold values from 0.5 to 1.5
- shift_mlp: bfloat16 [1024], P('fsdp'), may hold values from -4 to 4
- w_expand: bfloat16 [1024, 4096], P('fsdp'), may hold values from -0.1875 to 0.1875
- bias_expand: bfloat16 [4096], P('fsdp'), may hold values from -4 to 4
- w_contract: bfloat16 [4096, 1024], P('fsdp'), may hold values from -0.09375 to 0.09375
- bias_contract: bfloat16 [1024], P('fsdp'), may hold values from -4 to 4
- cotangent: bfloat16 [4, 2048, 1024], P('fsdp', 'ctx'), may hold values from -6 to 6
Outputs:
- block_out: bfloat16 [4, 2048, 1024], P('fsdp', 'ctx')
- grad_tokens: float32 [4, 2048, 1024], P('fsdp', 'ctx')
- grad_gain_attn: float32 [1024], P('fsdp')
- grad_shift_attn: float32 [1024], P('fsdp')
- grad_w_heads: float32 [1024, 3072], P('fsdp')
- grad_bias_query: float32 [1024], P('fsdp')
- grad_bias_value: float32 [1024], P('fsdp')
- grad_w_merge: float32 [1024, 1024], P('fsdp')
- grad_bias_merge: float32 [1024], P('fsdp')
- grad_gain_mlp: float32 [1024], P('fsdp')
- grad_shift_mlp: float32 [1024], P('fsdp')
- grad_w_expand: float32 [1024, 4096], P('fsdp')
- grad_bias_expand: float32 [4096], P('fsdp')
- grad_w_contract: float32 [4096, 1024], P('fsdp')
- grad_bias_contract: float32 [1024], P('fsdp')
All inputs are finite; a program needn't handle non-finite values.
Results may differ from a plain program's by a relative error of at most 0.018.
Values may be sent and summed in bfloat16 or wider, within the bound.
No kernel may reach another device: no remote copies, remote signals or barrier semaphores. Data moves between devices by JAX's collectives and lax.ppermute only.
A program may use at most 384 MiB of HBM per device.

v0:
```python
import math

import jax
import jax.numpy as jnp
from jax import lax
from jax.sharding import PartitionSpec as P

HEADS = 16
HEAD = 64


epsilon = 1e-05
masked_score = -1e30


def layer_norm(inputs, gain_vec, shift_vec):
    row_mean = jnp.mean(inputs, axis=-1, keepdims=True)
    centered = inputs - row_mean
    variance = jnp.mean(centered * centered, axis=-1, keepdims=True)
    return centered * lax.rsqrt(variance + epsilon) * gain_vec + shift_vec


def gelu_tanh(inputs):
    return jax.nn.gelu(inputs, approximate=True)


def dot_rows(left, right):
    return lax.dot_general(
        left, right, (((0,), (0,)), ((), ())), preferred_element_type=jnp.float32
    )


def dot_back(left, right):
    return lax.dot_general(
        left, right, (((1,), (1,)), ((), ())), preferred_element_type=jnp.float32
    )


def keep_state(state_in):
    return state_in


def in_blocks(pieces, step_fn, carried):
    width_rows = pieces[0].shape[1]
    block_rows = width_rows
    block_rows = 512
    nblocks = width_rows // block_rows

    def one_step(block_idx, carried_now):
        begin_row = block_idx * block_rows
        sliced = tuple(
            (lax.dynamic_slice_in_dim(member, begin_row, block_rows, 1) for member in pieces)
        )
        return step_fn(carried_now, sliced, begin_row)

    return lax.fori_loop(0, nblocks, one_step, carried)


def per_device(
    tokens_in,
    gain_attn,
    shift_attn,
    w_heads,
    bias_query,
    bias_value,
    w_merge,
    bias_merge,
    gain_mlp,
    shift_mlp,
    w_expand,
    bias_expand,
    w_contract,
    bias_contract,
    cotangent,
):
    gathered = (
        lax.all_gather(gain_attn, "fsdp", axis=0, tiled=True),
        lax.all_gather(shift_attn, "fsdp", axis=0, tiled=True),
        lax.all_gather(w_heads, "fsdp", axis=0, tiled=True),
        lax.all_gather(bias_query, "fsdp", axis=0, tiled=True),
        lax.all_gather(bias_value, "fsdp", axis=0, tiled=True),
        lax.all_gather(w_merge, "fsdp", axis=0, tiled=True),
        lax.all_gather(bias_merge, "fsdp", axis=0, tiled=True),
        lax.all_gather(gain_mlp, "fsdp", axis=0, tiled=True),
        lax.all_gather(shift_mlp, "fsdp", axis=0, tiled=True),
        lax.all_gather(w_expand, "fsdp", axis=0, tiled=True),
        lax.all_gather(bias_expand, "fsdp", axis=0, tiled=True),
        lax.all_gather(w_contract, "fsdp", axis=0, tiled=True),
        lax.all_gather(bias_contract, "fsdp", axis=0, tiled=True),
    )
    (
        gain_one,
        shift_one,
        heads_full,
        query_bias,
        value_bias,
        merge_full,
        merge_bias,
        gain_two,
        shift_two,
        expand_full,
        expand_bias,
        contract_full,
        contract_bias,
    ) = gathered
    seq_here, group_rows, model_width = tokens_in.shape
    row_count = seq_here * group_rows
    scale_now = 1.0 / math.sqrt(HEAD)
    my_first = lax.axis_index("ctx") * group_rows
    q_pos = my_first + jnp.arange(group_rows, dtype=jnp.int32)
    head_shape = (seq_here, group_rows, HEADS, HEAD)
    seq_shape = (seq_here, group_rows, model_width)
    residual_in = tokens_in.reshape(row_count, model_width).astype(jnp.float32)
    normed_one, pull_one = jax.vjp(
        layer_norm, residual_in, gain_one.astype(jnp.float32), shift_one.astype(jnp.float32)
    )
    normed_one_b = normed_one.astype(jnp.bfloat16)
    projected = jnp.dot(normed_one_b, heads_full, preferred_element_type=jnp.float32)
    query_rows = (projected[:, :model_width] + query_bias).astype(jnp.bfloat16)
    key_rows = projected[:, model_width : 2 * model_width].astype(jnp.bfloat16)
    value_rows = (projected[:, 2 * model_width :] + value_bias).astype(jnp.bfloat16)
    query_heads = query_rows.reshape(head_shape)
    key_heads = key_rows.reshape(head_shape)
    value_heads = value_rows.reshape(head_shape)
    key_seq = key_rows.reshape(seq_shape)
    value_seq = value_rows.reshape(seq_shape)

    def attend_step(carried, pieces, offset):
        key_part, value_part = pieces
        n_keys = key_part.shape[1]
        key_piece = key_part.reshape(seq_here, n_keys, HEADS, HEAD)
        value_piece = value_part.reshape(seq_here, n_keys, HEADS, HEAD)
        key_idx = offset + jnp.arange(n_keys, dtype=jnp.int32)
        allowed = (key_idx[None, :] <= q_pos[:, None])[None, None]

        def attend_compute(state_in):
            row_top, totals, accumulated = state_in
            scores = (
                jnp.einsum(
                    "sqhe,skhe->shqk", query_heads, key_piece, preferred_element_type=jnp.float32
                )
                * scale_now
            )
            masked = jnp.where(allowed, scores, masked_score)
            new_top = jnp.maximum(row_top, jnp.max(masked, axis=-1))
            factor = jnp.exp(row_top - new_top)
            weights = jnp.where(allowed, jnp.exp(masked - new_top[..., None]), 0.0)
            totals = totals * factor + jnp.sum(weights, axis=-1)
            accumulated = accumulated * factor[..., None] + jnp.einsum(
                "shqk,skhe->shqe",
                weights.astype(jnp.bfloat16),
                value_piece,
                preferred_element_type=jnp.float32,
            )
            return (new_top, totals, accumulated)

        return lax.cond(offset <= q_pos[-1], attend_compute, keep_state, carried)

    stat_shape = (seq_here, HEADS, group_rows)
    initial = (
        jnp.full(stat_shape, masked_score, jnp.float32),
        jnp.zeros(stat_shape, jnp.float32),
        jnp.zeros((seq_here, HEADS, group_rows, HEAD), jnp.float32),
    )
    row_top, totals, accumulated = in_blocks(
        (
            lax.all_gather(key_seq, "ctx", axis=1, tiled=True),
            lax.all_gather(value_seq, "ctx", axis=1, tiled=True),
        ),
        attend_step,
        initial,
    )
    mixed_heads = accumulated / totals[..., None]
    mixed_f = jnp.transpose(mixed_heads, (0, 2, 1, 3)).reshape(row_count, model_width)
    log_sum = row_top + jnp.log(totals)
    mixed_b = mixed_f.astype(jnp.bfloat16)
    merged = jnp.dot(mixed_b, merge_full, preferred_element_type=jnp.float32) + merge_bias
    middle = residual_in + merged
    normed_two, pull_two = jax.vjp(
        layer_norm, middle, gain_two.astype(jnp.float32), shift_two.astype(jnp.float32)
    )
    normed_two_b = normed_two.astype(jnp.bfloat16)
    inner_pre = jnp.dot(normed_two_b, expand_full, preferred_element_type=jnp.float32) + expand_bias
    active, pull_gelu = jax.vjp(gelu_tanh, inner_pre)
    active_b = active.astype(jnp.bfloat16)
    result = (
        middle
        + jnp.dot(active_b, contract_full, preferred_element_type=jnp.float32)
        + contract_bias
    )
    block_out = result.astype(jnp.bfloat16).reshape(seq_shape)
    heads_back, merge_back, expand_back, contract_back = (
        heads_full,
        merge_full,
        expand_full,
        contract_full,
    )
    upstream = cotangent.reshape(row_count, model_width)
    upstream_f = upstream.astype(jnp.float32)
    grad_contract_bias = jnp.sum(upstream_f, axis=0)
    grad_contract = dot_rows(active_b, upstream)
    grad_active = dot_back(upstream, contract_back)
    grad_inner = pull_gelu(grad_active)[0].astype(jnp.bfloat16)
    grad_expand_bias = jnp.sum(grad_inner.astype(jnp.float32), axis=0)
    grad_expand = dot_rows(normed_two_b, grad_inner)
    grad_normed_two = dot_back(grad_inner, expand_back)
    grad_middle_part, grad_gain_two, grad_shift_two = pull_two(grad_normed_two)
    grad_middle = upstream_f + grad_middle_part
    grad_merged = grad_middle.astype(jnp.bfloat16)
    grad_merge_bias = jnp.sum(grad_merged.astype(jnp.float32), axis=0)
    grad_merge = dot_rows(mixed_b, grad_merged)
    grad_mixed = dot_back(grad_merged, merge_back).astype(jnp.bfloat16)
    grad_mixed_heads = grad_mixed.reshape(head_shape)
    delta_rows = jnp.sum((grad_mixed.astype(jnp.float32) * mixed_f).reshape(head_shape), axis=-1)
    delta_heads = jnp.transpose(delta_rows, (0, 2, 1))
    log_sum_rows = jnp.transpose(log_sum, (0, 2, 1))

    def query_step(carried, pieces, offset):
        key_part, value_part = pieces
        n_keys = key_part.shape[1]
        key_piece = key_part.reshape(seq_here, n_keys, HEADS, HEAD)
        value_piece = value_part.reshape(seq_here, n_keys, HEADS, HEAD)
        key_idx = offset + jnp.arange(n_keys, dtype=jnp.int32)
        allowed = (key_idx[None, :] <= q_pos[:, None])[None, None]

        def query_compute(grad_in):
            scores = (
                jnp.einsum(
                    "sqhe,skhe->shqk", query_heads, key_piece, preferred_element_type=jnp.float32
                )
                * scale_now
            )
            probabilities = jnp.where(allowed, jnp.exp(scores - log_sum[..., None]), 0.0)
            grad_prob = jnp.einsum(
                "sqhe,skhe->shqk", grad_mixed_heads, value_piece, preferred_element_type=jnp.float32
            )
            dscore = (probabilities * (grad_prob - delta_heads[..., None])).astype(jnp.bfloat16)
            return (
                grad_in
                + jnp.einsum(
                    "shqk,skhe->shqe", dscore, key_piece, preferred_element_type=jnp.float32
                )
                * scale_now
            )

        return lax.cond(offset <= q_pos[-1], query_compute, keep_state, carried)

    heads_zero = jnp.zeros((seq_here, HEADS, group_rows, HEAD), jnp.float32)
    grad_query_heads = in_blocks(
        (
            lax.all_gather(key_seq, "ctx", axis=1, tiled=True),
            lax.all_gather(value_seq, "ctx", axis=1, tiled=True),
        ),
        query_step,
        heads_zero,
    )
    stats_all = (
        lax.all_gather(log_sum_rows, "ctx", axis=1, tiled=True),
        lax.all_gather(delta_rows, "ctx", axis=1, tiled=True),
    )

    def owner_step(carried, pieces, offset):
        query_part, grad_part = pieces
        n_rows = query_part.shape[1]
        q_piece = query_part.reshape(seq_here, n_rows, HEADS, HEAD)
        g_piece = grad_part.reshape(seq_here, n_rows, HEADS, HEAD)
        lse_piece = jnp.transpose(
            lax.dynamic_slice_in_dim(stats_all[0], offset, n_rows, 1), (0, 2, 1)
        )
        delta_piece = jnp.transpose(
            lax.dynamic_slice_in_dim(stats_all[1], offset, n_rows, 1), (0, 2, 1)
        )
        row_idx = offset + jnp.arange(n_rows, dtype=jnp.int32)
        allowed = (q_pos[None, :] <= row_idx[:, None])[None, None]

        def owner_compute(state_in):
            grad_key, grad_value = state_in
            scores = (
                jnp.einsum(
                    "sqhe,skhe->shqk", q_piece, key_heads, preferred_element_type=jnp.float32
                )
                * scale_now
            )
            probabilities = jnp.where(allowed, jnp.exp(scores - lse_piece[..., None]), 0.0)
            grad_prob = jnp.einsum(
                "sqhe,skhe->shqk", g_piece, value_heads, preferred_element_type=jnp.float32
            )
            dscore = (probabilities * (grad_prob - delta_piece[..., None])).astype(jnp.bfloat16)
            grad_value = grad_value + jnp.einsum(
                "shqk,sqhe->shke",
                probabilities.astype(jnp.bfloat16),
                g_piece,
                preferred_element_type=jnp.float32,
            )
            grad_key = (
                grad_key
                + jnp.einsum("shqk,sqhe->shke", dscore, q_piece, preferred_element_type=jnp.float32)
                * scale_now
            )
            return (grad_key, grad_value)

        return lax.cond(offset + n_rows - 1 >= my_first, owner_compute, keep_state, carried)

    query_seq = query_rows.reshape(seq_shape)
    grad_seq = grad_mixed.reshape(seq_shape)
    grad_key_heads, grad_value_heads = in_blocks(
        (
            lax.all_gather(query_seq, "ctx", axis=1, tiled=True),
            lax.all_gather(grad_seq, "ctx", axis=1, tiled=True),
        ),
        owner_step,
        (heads_zero, heads_zero),
    )

    def to_rows(heads_arr):
        return (
            jnp.transpose(heads_arr, (0, 2, 1, 3))
            .reshape(row_count, model_width)
            .astype(jnp.bfloat16)
        )

    grad_query_rows = to_rows(grad_query_heads)
    grad_value_rows = to_rows(grad_value_heads)
    grad_proj = jnp.concatenate((grad_query_rows, to_rows(grad_key_heads), grad_value_rows), axis=1)
    grad_heads = dot_rows(normed_one_b, grad_proj)
    grad_query_bias = jnp.sum(grad_query_rows.astype(jnp.float32), axis=0)
    grad_value_bias = jnp.sum(grad_value_rows.astype(jnp.float32), axis=0)
    grad_normed_one = dot_back(grad_proj, heads_back)
    grad_in_part, grad_gain_one, grad_shift_one = pull_one(grad_normed_one)
    grad_tokens = (grad_middle + grad_in_part).reshape(seq_shape)
    halves = (
        lax.psum_scatter(grad_gain_one, "fsdp", scatter_dimension=0, tiled=True),
        lax.psum_scatter(grad_shift_one, "fsdp", scatter_dimension=0, tiled=True),
        lax.psum_scatter(grad_heads, "fsdp", scatter_dimension=0, tiled=True),
        lax.psum_scatter(grad_query_bias, "fsdp", scatter_dimension=0, tiled=True),
        lax.psum_scatter(grad_value_bias, "fsdp", scatter_dimension=0, tiled=True),
        lax.psum_scatter(grad_merge, "fsdp", scatter_dimension=0, tiled=True),
        lax.psum_scatter(grad_merge_bias, "fsdp", scatter_dimension=0, tiled=True),
        lax.psum_scatter(grad_gain_two, "fsdp", scatter_dimension=0, tiled=True),
        lax.psum_scatter(grad_shift_two, "fsdp", scatter_dimension=0, tiled=True),
        lax.psum_scatter(grad_expand, "fsdp", scatter_dimension=0, tiled=True),
        lax.psum_scatter(grad_expand_bias, "fsdp", scatter_dimension=0, tiled=True),
        lax.psum_scatter(grad_contract, "fsdp", scatter_dimension=0, tiled=True),
        lax.psum_scatter(grad_contract_bias, "fsdp", scatter_dimension=0, tiled=True),
    )
    summed = lax.psum(
        (
            halves[0],
            halves[1],
            halves[2],
            halves[3],
            halves[4],
            halves[5],
            halves[6],
            halves[7],
            halves[8],
            halves[9],
            halves[10],
            halves[11],
            halves[12],
        ),
        "ctx",
    )
    return (
        block_out,
        grad_tokens,
        summed[0],
        summed[1],
        summed[2],
        summed[3],
        summed[4],
        summed[5],
        summed[6],
        summed[7],
        summed[8],
        summed[9],
        summed[10],
        summed[11],
        summed[12],
    )


def solution(mesh):
    placed = (
        P("fsdp", "ctx", None),
        P("fsdp"),
        P("fsdp"),
        P("fsdp", None),
        P("fsdp"),
        P("fsdp"),
        P("fsdp", None),
        P("fsdp"),
        P("fsdp"),
        P("fsdp"),
        P("fsdp", None),
        P("fsdp"),
        P("fsdp", None),
        P("fsdp"),
        P("fsdp", "ctx", None),
    )
    return jax.shard_map(
        per_device,
        mesh=mesh,
        in_specs=placed,
        out_specs=(
            P("fsdp", "ctx", None),
            P("fsdp", "ctx", None),
            P("fsdp"),
            P("fsdp"),
            P("fsdp", None),
            P("fsdp"),
            P("fsdp"),
            P("fsdp", None),
            P("fsdp"),
            P("fsdp"),
            P("fsdp"),
            P("fsdp", None),
            P("fsdp"),
            P("fsdp", None),
            P("fsdp"),
        ),
        check_vma=False,
    )
```

profile of v0, /device:TPU:0, one launch (start us, length us, event | category | flops | bytes accessed | tf_op | source)
XLA Modules:
  0.0 1716.1 jit_solution(2156204956828630098)
XLA Ops:
  8.8 5.2 all-gather.1
  19.2 73.5 %all-gather.17.cloned.1.call-done = bf16[1024,3072]{1,0:T(8,128)(2,1)} async-done(((bf16[512,3072]{1,0:T(8,128)(2,1)}), bf16[1024,3072]{1,0:T(8,128)(2,1)}) %all-gather.17.cloned.1.call-update) | async-done | bytes 6291472 | tf_op jit(solution)/shard_map/all_gather | solution.py:79
  92.7 4.6 fusion.76
  133.4 65.1 %all-gather.27.cloned.1.call-done = bf16[4096,1024]{1,0:T(8,128)(2,1)} async-done(((bf16[2048,1024]{1,0:T(8,128)(2,1)}), bf16[4096,1024]{1,0:T(8,128)(2,1)}) %all-gather.27.cloned.1.call-update) | async-done | bytes 8388624 | tf_op jit(solution)/shard_map/all_gather | solution.py:88
  198.5 7.8 fusion.77
  206.3 73.1 %all-gather.19.cloned.1.call-done = bf16[2,2048,1024]{1,2,0:T(8,128)(2,1)} async-done(((bf16[2,128,1024]{1,2,0:T(8,128)(2,1)}), bf16[2,2048,1024]{1,2,0:T(8,128)(2,1)}) %all-gather.19.cloned.1.call-update) | async-done | bytes 8388624 | tf_op jit(solution)/shard_map/all_gather | solution.py:167
  279.4 78.9 %all-gather.21.cloned.1.call-done = bf16[2,2048,1024]{1,2,0:T(8,128)(2,1)} async-done(((bf16[2,128,1024]{1,2,0:T(8,128)(2,1)}), bf16[2,2048,1024]{1,2,0:T(8,128)(2,1)}) %all-gather.21.cloned.1.call-update) | async-done | bytes 8388624 | tf_op jit(solution)/shard_map/all_gather | solution.py:168
  358.4 14.9 while.54
  359.9 9.6 conditional.8
  375.6 15.3 all-gather.23.cloned.1.call-done
  393.7 102.7 %all-gather.25.cloned.1.call-done = bf16[1024,4096]{1,0:T(8,128)(2,1)} async-done(((bf16[512,4096]{1,0:T(8,128)(2,1)}), bf16[1024,4096]{1,0:T(8,128)(2,1)}) %all-gather.25.cloned.1.call-update) | async-done | bytes 8388624 | tf_op jit(solution)/shard_map/all_gather | solution.py:86
  496.4 12.9 convert_reduce_fusion
  522.6 10.0 fusion.67
  532.7 11.5 fusion.68
  562.4 23.3 %while.55 = (s32[]{:T(128)}, f32[2,16,128,64]{2,3,1,0:T(8,128)}, s32[128]{0:T(128)S(1)}, bf16[2,2048,1024]{1,2,0:T(8,128)(2,1)}, bf16[2,128,16,64]{1,3,2,0:T(8,1...) while((s32[]{:T(128)}, f32[2,16,128,64]{2,3,1,0:T(8,128)}, ...), condition=%wide.region_16.17_spmd, body=%wide.region_13.16_spmd.sunk | while | flops 818479616 | bytes 34775832 | solution.py:56
  563.6 18.2 %conditional.9 = (f32[2,16,128,64]{2,3,1,0:T(8,128)}) conditional(s32[]{:T(128)} %convert_element_type.294, f32[2,16,128,64]{2,3,1,0:T(8,128)} %get-tuple-element.1522, (s32[]{:T(128)}, s32[1,512]{1,0:T(1,128)S(1)}, s32[128]{0:T(128)S(1)}, bf16[2,2048,1024]{1,2,0:T(8,128)(2,1)}, bf16[2,128,16,64]{1,3,2,0:T(8,128)(2,1)S(1)}, ...), branch_computations={%region_14.14_spmd, %region_15.15_spmd} | conditional | flops 818479616 | bytes 34773552 | solution.py:246
  567.6 4.7 fusion.74
  572.5 9.3 fusion.23
  587.7 75.7 %all_gather.75 = f32[2,2048,16]{1,0,2:T(2,128)S(1)} all-gather(f32[2,128,16]{1,0,2:T(2,128)S(1)} %reduce_sum.216), channel_id=1, replica_groups=mesh['ctx'=16,'fsdp'=2] {'ctx'}, dimensions={1}, use_global_device_ids=true | all-gather | bytes 278528 | tf_op jit(solution)/shard_map/all_gather | solution.py:259
  663.4 19.3 %all_gather.74 = f32[2,2048,16]{1,2,0:T(8,128)S(1)} all-gather(f32[2,128,16]{1,2,0:T(8,128)S(1)} %bitcast.212), channel_id=1, replica_groups=mesh['ctx'=16,'fsdp'=2] {'ctx'}, dimensions={1}, use_global_device_ids=true | all-gather | bytes 278528 | tf_op jit(solution)/shard_map/all_gather | solution.py:258
  684.8 105.3 %while.56 = (s32[]{:T(128)}, f32[2,16,128,64]{2,3,1,0:T(8,128)S(1)}, f32[2,16,128,64]{2,3,1,0:T(8,128)}, s32[]{:T(128)}, f32[2,2048,16]{1,2,0:T(8,128)S(1)}, /*i...) while((s32[]{:T(128)}, ...), condition=%wide.region_20.21_spmd.clone.clone, body=%wide.region_17.20_spmd.clone.clone.sunk | while | flops 1095565952 | bytes 56371640 | solution.py:56
  684.9 26.1 %conditional.10 = ((f32[2,16,128,64]{2,3,1,0:T(8,128)S(1)}, f32[2,16,128,64]{2,3,1,0:T(8,128)})) conditional(s32[]{:T(128)} %convert_element_type.295, (f32[2,16,128,64]{2,3,1,0:T(8,128)S(1)}, f32[2,16,128,64]{2,3,1,0:T(8,128)}) %tuple.196, (s32[]{:T(128)}, s32[]{:T(128)}, s32[512,1]{0,1:T(1,128)S(1)}, bf16[2,2048,1024]{1,2,0:T(8,128)(2,1)}, ...), branch_computations={%region_18.18_spmd, %region_19.19_spmd} | conditional | flops 1095565952 | bytes 55975516 | solution.py:302
  689.9 4.7 fusion.75
  694.7 9.7 fusion.40
  704.4 6.6 fusion.41
  711.1 26.1 %conditional.10 = ((f32[2,16,128,64]{2,3,1,0:T(8,128)S(1)}, f32[2,16,128,64]{2,3,1,0:T(8,128)})) conditional(s32[]{:T(128)} %convert_element_type.295, (f32[2,16,128,64]{2,3,1,0:T(8,128)S(1)}, f32[2,16,128,64]{2,3,1,0:T(8,128)}) %tuple.196, (s32[]{:T(128)}, s32[]{:T(128)}, s32[512,1]{0,1:T(1,128)S(1)}, bf16[2,2048,1024]{1,2,0:T(8,128)(2,1)}, ...), branch_computations={%region_18.18_spmd, %region_19.19_spmd} | conditional | flops 1095565952 | bytes 55975516 | solution.py:302
  716.1 4.7 fusion.75
  721.0 9.8 fusion.40
  730.7 6.5 fusion.41
  737.4 26.3 %conditional.10 = ((f32[2,16,128,64]{2,3,1,0:T(8,128)S(1)}, f32[2,16,128,64]{2,3,1,0:T(8,128)})) conditional(s32[]{:T(128)} %convert_element_type.295, (f32[2,16,128,64]{2,3,1,0:T(8,128)S(1)}, f32[2,16,128,64]{2,3,1,0:T(8,128)}) %tuple.196, (s32[]{:T(128)}, s32[]{:T(128)}, s32[512,1]{0,1:T(1,128)S(1)}, bf16[2,2048,1024]{1,2,0:T(8,128)(2,1)}, ...), branch_computations={%region_18.18_spmd, %region_19.19_spmd} | conditional | flops 1095565952 | bytes 55975516 | solution.py:302
  742.3 4.7 fusion.75
  747.2 9.6 fusion.40
  756.8 6.8 fusion.41
  763.7 26.5 %conditional.10 = ((f32[2,16,128,64]{2,3,1,0:T(8,128)S(1)}, f32[2,16,128,64]{2,3,1,0:T(8,128)})) conditional(s32[]{:T(128)} %convert_element_type.295, (f32[2,16,128,64]{2,3,1,0:T(8,128)S(1)}, f32[2,16,128,64]{2,3,1,0:T(8,128)}) %tuple.196, (s32[]{:T(128)}, s32[]{:T(128)}, s32[512,1]{0,1:T(1,128)S(1)}, bf16[2,2048,1024]{1,2,0:T(8,128)(2,1)}, ...), branch_computations={%region_18.18_spmd, %region_19.19_spmd} | conditional | flops 1095565952 | bytes 55975516 | solution.py:302
  768.7 4.7 fusion.75
  773.5 9.9 fusion.40
  783.4 6.8 fusion.41
  794.3 6.4 fusion.78
  800.8 103.2 %reduce-scatter.9.cloned.1.call-done = f32[512,4096]{1,0:T(8,128)} async-done(((f32[1024,4096]{1,0:T(8,128)}), f32[512,4096]{1,0:T(8,128)}) %reduce-scatter.9.cloned.1.call-update) | async-done | bytes 8388624 | tf_op jit(solution)/shard_map/reduce_scatter | solution.py:341
  904.0 191.5 %reduce-scatter.11.cloned.1.call-done = f32[2048,1024]{1,0:T(8,128)} async-done(((f32[4096,1024]{1,0:T(8,128)}), f32[2048,1024]{1,0:T(8,128)}) %reduce-scatter.11.cloned.1.call-update) | async-done | bytes 8388624 | tf_op jit(solution)/shard_map/reduce_scatter | solution.py:343
  1095.5 146.8 %reduce-scatter.5.cloned.1.call-done = f32[512,3072]{1,0:T(8,128)} async-done(((f32[1024,3072]{1,0:T(8,128)}), f32[512,3072]{1,0:T(8,128)}) %reduce-scatter.5.cloned.1.call-update) | async-done | bytes 6291472 | tf_op jit(solution)/shard_map/reduce_scatter | solution.py:334
  1242.9 4.6 all-gather.7
  1249.6 9.1 fusion.57
  1258.9 5.5 fusion.69
  1265.0 7.3 all-reduce.11
  1273.0 62.0 %all-reduce.9 = (f32[512]{0:T(512)}, f32[512]{0:T(512)}, f32[512]{0:T(512)}, f32[512]{0:T(512)}, f32[512]{0:T(512)}, /*index=5*/f32[512]{0:T(512)}, f32[512]{0:T(512)}, f32[2048]{0:T(1024)}, f32[512]{0:T(512)}) all-reduce(f32[512]{0:T(512)S(1)} %dynamic-slice.1, ...), channel_id=1, replica_groups=mesh['ctx'=16,'fsdp'=2] {'ctx'}, use_global_device_ids=true, to_apply=%region_25.26 | all-reduce | flops 6144 | bytes 49152 | tf_op jit(solution)/shard_map/psum | solution.py:346
  1336.4 355.0 %all-reduce.14.cloned.1.call-done = (f32[512,3072]{1,0:T(8,128)}, f32[512,1024]{1,0:T(8,128)}, f32[512,4096]{1,0:T(8,128)}, f32[2048,1024]{1,0:T(8,128)}) async-done(((f32[512,3072]{1,0:T(8,128)}, f32[512,1024]{1,0:T(8,128)}, f32[512,4096]{1,0:T(8,128)}, f32[2048,1024]{1,0:T(8,128)}), (f32[512,3072]{1,0:T(8,128)}, f32[512,1024]{1,0:T(8,128)}, f32[512,4096]{1,0:T(8,128)}, ...) | async-done | bytes 25165840 | tf_op jit(solution)/shard_map/psum | solution.py:346
  1691.4 6.9 copy.158
  (316 shorter events, 141.1 us)
Async XLA Ops:
  7.2 6.8 copy-start.44
  7.2 11.2 copy-start
  7.2 85.5 %all-gather.17.cloned.1.call-start = ((), (), s32[]{:S(2)}) async-start(), calls=%async_computation.4 | async-start | bytes 9437184 | tf_op jit(solution)/shard_map/all_gather | solution.py:79
  7.9 190.6 %all-gather.27.cloned.1.call-start = ((), (), s32[]{:S(2)}) async-start(), calls=%async_computation.9 | async-start | bytes 12582912 | tf_op jit(solution)/shard_map/all_gather | solution.py:88
  8.7 270.7 %all-gather.19.cloned.1.call-start = ((), (), s32[]{:S(2)}) async-start(), calls=%async_computation.5 | async-start | bytes 8912896 | tf_op jit(solution)/shard_map/all_gather | solution.py:167
  18.4 78.9 %copy-start.28 = (f32[2,1,512]{2,1,0:T(1,128)}, f32[2,1,512]{2,1,0:T(1,128)S(1)}, u32[]{:S(2)}) copy-start(f32[2,1,512]{2,1,0:T(1,128)S(1)} %convert_element_type.212) | copy-start | bytes 12292
  18.5 78.8 %copy-start.32 = (f32[256]{0:T(256)}, f32[256]{0:T(256)S(1)}, u32[]{:S(2)}) copy-start(f32[256]{0:T(256)S(1)} %get-tuple-element.1281) | copy-start | bytes 3076
  18.8 78.5 %copy-start.38 = (f32[2,128]{1,0:T(2,128)}, f32[2,128]{1,0:T(2,128)S(1)}, u32[]{:S(2)}) copy-start(f32[2,128]{1,0:T(2,128)S(1)} %multiply_reduce_fusion.5) | copy-start | bytes 3076
  18.8 78.5 %copy-start.34 = (f32[256]{0:T(256)}, f32[256]{0:T(256)S(1)}, u32[]{:S(2)}) copy-start(f32[256]{0:T(256)S(1)} %bitcast_rsqrt_fusion) | copy-start | bytes 3076
  19.1 73.5 %copy-start.24 = (bf16[256,1024]{1,0:T(8,128)(2,1)}, bf16[256,1024]{1,0:T(8,128)(2,1)S(1)}, u32[]{:S(2)}) copy-start(bf16[256,1024]{1,0:T(8,128)(2,1)S(1)} %add_convert_fusion.1) | copy-start | bytes 1572868
  19.2 81.0 %copy-start.45 = (bf16[512]{0:T(512)(128)(2,1)S(1)}, bf16[512]{0:T(512)(128)(2,1)}, u32[]{:S(2)}) copy-start(bf16[512]{0:T(512)(128)(2,1)} %param.32) | copy-start | bytes 3076
  19.2 85.3 %copy-start.46 = (bf16[512]{0:T(512)(128)(2,1)S(1)}, bf16[512]{0:T(512)(128)(2,1)}, u32[]{:S(2)}) copy-start(bf16[512]{0:T(512)(128)(2,1)} %param.31) | copy-start | bytes 3076
  99.1 14.1 copy-start.12
  100.1 258.2 %all-gather.21.cloned.1.call-start = ((), (), s32[]{:S(2)}) async-start(), calls=%async_computation.6 | async-start | bytes 8912896 | tf_op jit(solution)/shard_map/all_gather | solution.py:168
  110.9 7.8 copy-start.40
  110.9 12.2 copy-start.48
  110.9 16.5 copy-start.49
  112.0 279.0 %all-gather.23.cloned.1.call-start = ((), (), s32[]{:S(2)}) async-start(), calls=%async_computation.7 | async-start | bytes 3145728 | tf_op jit(solution)/shard_map/all_gather | solution.py:82
  112.6 85.9 %copy-start.7 = (bf16[2,128,1024]{2,1,0:T(8,128)(2,1)S(1)}, bf16[2,128,1024]{2,1,0:T(8,128)(2,1)}, u32[]{:S(2)}) copy-start(bf16[2,128,1024]{2,1,0:T(8,128)(2,1)} %param.41) | copy-start | bytes 1572868
  112.6 383.8 %all-gather.25.cloned.1.call-start = ((), (), s32[]{:S(2)}) async-start(), calls=%async_computation.8 | async-start | bytes 12582912 | tf_op jit(solution)/shard_map/all_gather | solution.py:86
  113.2 570.4 %all-gather.29.cloned.1.call-start = ((), (), s32[]{:S(2)}) async-start(), calls=%async_computation.10 | async-start | bytes 8912896 | tf_op jit(solution)/shard_map/all_gather | solution.py:308
  114.2 569.4 %all-gather.31.cloned.1.call-start = ((), (), s32[]{:S(2)}) async-start(), calls=%async_computation.11 | async-start | bytes 8912896 | tf_op jit(solution)/shard_map/all_gather | solution.py:309
  393.4 129.2 %copy-start.2 = (f32[256,1024]{1,0:T(8,128)}, f32[256,1024]{1,0:T(8,128)S(1)}, u32[]{:S(2)}) copy-start(f32[256,1024]{1,0:T(8,128)S(1)} %get-tuple-element.1284) | copy-start | bytes 3145732
  496.4 12.9 copy-start.51
  518.7 282.1 %reduce-scatter.7.cloned.1.call-start = ((), (), s32[]{:S(2)}) async-start(), calls=%async_computation.13 | async-start | bytes 6291456 | tf_op jit(solution)/shard_map/reduce_scatter | solution.py:337
  522.6 381.5 %reduce-scatter.9.cloned.1.call-start = ((), (), s32[]{:S(2)}) async-start(), calls=%async_computation.14 | async-start | bytes 25165824 | tf_op jit(solution)/shard_map/reduce_scatter | solution.py:341
  532.6 562.9 %reduce-scatter.11.cloned.1.call-start = ((), (), s32[]{:S(2)}) async-start(), calls=%async_computation.15 | async-start | bytes 25165824 | tf_op jit(solution)/shard_map/reduce_scatter | solution.py:343
  544.2 9.2 copy-start.11
  544.2 698.0 %reduce-scatter.5.cloned.1.call-start = ((), (), s32[]{:S(2)}) async-start(), calls=%async_computation.12 | async-start | bytes 18874368 | tf_op jit(solution)/shard_map/reduce_scatter | solution.py:334
  548.5 9.3 copy-start.17
  704.4 6.6 copy-start.20
  730.7 6.5 copy-start.20
  756.8 6.8 copy-start.20
  783.4 6.8 copy-start.20
  800.7 890.6 %all-reduce.14.cloned.1.call-start = ((), (), s32[]{:S(2)}) async-start(), calls=%async_computation.16 | async-start | bytes 50331648 | tf_op jit(solution)/shard_map/psum | solution.py:346
  1242.3 7.2 copy-start.9
  1242.3 7.3 copy-start.3
  1249.6 9.2 copy-start.1
  1249.6 9.2 copy-start.29
  1249.6 9.2 copy-start.33
  1258.8 6.1 copy-start.30
  1258.9 6.1 copy-start.31
  1258.9 6.1 copy-start.41
  1258.9 6.1 copy-start.42
  1258.9 76.0 %copy-start.5 = (f32[256,1024]{1,0:T(8,128)S(1)}, f32[256,1024]{1,0:T(8,128)}, u32[]{:S(2)}) copy-start(f32[256,1024]{1,0:T(8,128)} %copy-done.4) | copy-start | bytes 3145732
  1258.9 76.0 %copy-start.37 = (f32[256]{0:T(256)S(1)}, f32[256]{0:T(256)}, u32[]{:S(2)}) copy-start(f32[256]{0:T(256)} %copy-done.36) | copy-start | bytes 3076
  1691.4 6.9 copy-start.26
  1691.4 8.6 copy-start.10
  (26 other events, 73.3 us)
Sparse Core Ops, SparseCore 0:
  9.6 83.0 all-gather.16
  94.2 104.2 all-gather.26
  201.2 78.0 all-gather.18
  282.0 76.2 all-gather.20
  359.7 31.2 all-gather.22
  392.4 103.9 all-gather.24
  498.6 78.1 all-gather.28
  578.9 77.9 all-gather.30
  659.8 52.7 reduce-scatter.6
  714.8 189.1 reduce-scatter.8
  906.3 189.1 reduce-scatter.10
  1097.7 144.4 reduce-scatter.4
  1247.9 443.4 all-reduce.13
where the time goes:
time: 1720 us
  waiting for transfers between devices  1210 us (70%)
  blocking collectives  205 us (12%)
  matrix products  182 us (11%)
  local copies, waits for them, and re-layouts  85.3 us (5%)
    psum x1, waiting for transfers between devices, per_device(): lax.psum((halves[0], halves[1], halves[2], halves[3], halves[4], halves[5...  355 us
    reduce_scatter x1, waiting for transfers between devices, per_device(): lax.psum_scatter(grad_contract, 'fsdp', scatter_dimension=0, tiled=True)  191 us
    reduce_scatter x1, waiting for transfers between devices, per_device(): lax.psum_scatter(grad_heads, 'fsdp', scatter_dimension=0, tiled=True)  147 us
    reduce_scatter x1, waiting for transfers between devices, per_device(): lax.psum_scatter(grad_expand, 'fsdp', scatter_dimension=0, tiled=True)  103 us
    all_gather x1, waiting for transfers between devices, per_device(): lax.all_gather(w_expand, 'fsdp', axis=0, tiled=True)  103 us
    all_gather x1, waiting for transfers between devices, per_device(): lax.all_gather(value_seq, 'ctx', axis=1, tiled=True)  78.9 us
    all_gather x1, blocking collectives, per_device(): lax.all_gather(delta_rows, 'ctx', axis=1, tiled=True)  75.7 us
    all_gather x1, waiting for transfers between devices, per_device(): lax.all_gather(w_heads, 'fsdp', axis=0, tiled=True)  73.5 us
  transfers between devices with their start and end apart: 13, of which 10 were waited for; matrix products, arithmetic and copies ran while one was open for 15% of the time, Pallas kernels for 0%

commit v1 on v0

v1 whole, which is shorter than its diff:
```python
import functools
import math

import jax
import jax.numpy as jnp
from jax import lax
from jax.experimental import pallas as pl
from jax.experimental.pallas import tpu as pltpu
from jax.sharding import PartitionSpec as P

HEAD = 64
EPS = 1e-05
LOWEST = -1e30
GELU_A = math.sqrt(2.0 / math.pi)
GELU_B = 0.044715
F32 = jnp.float32
BF16 = jnp.bfloat16
VMEM_BYTES = 52 * 1024 * 1024
GAIN_ATTN, SHIFT_ATTN, BIAS_QUERY, BIAS_VALUE = 0, 1, 2, 3
BIAS_MERGE, GAIN_MLP, SHIFT_MLP, BIAS_CONTRACT = 4, 5, 6, 7
BIAS_EXPAND = 8


def mm(left, right):
    return jnp.dot(left, right, preferred_element_type=F32)


def mm_nt(left, right):
    return lax.dot_general(left, right, (((1,), (1,)), ((), ())), preferred_element_type=F32)


def mm_tn(left, right):
    return lax.dot_general(left, right, (((0,), (0,)), ((), ())), preferred_element_type=F32)


def params(**extra):
    return pltpu.CompilerParams(vmem_limit_bytes=VMEM_BYTES, **extra)


def cost(flops, nbytes, trans=0):
    return pl.CostEstimate(flops=int(flops), bytes_accessed=int(nbytes), transcendentals=int(trans))


def whole(shape):
    return pl.BlockSpec(shape, lambda *_: (0,) * len(shape))


def full_row(at, mine_ref, theirs_ref, row):
    mine = mine_ref[row : row + 1, :].astype(F32)
    theirs = theirs_ref[row : row + 1, :].astype(F32)
    low = jnp.where(at == 0, mine, theirs)
    high = jnp.where(at == 0, theirs, mine)
    return jnp.concatenate([low, high], axis=1)


def normalise(rows):
    mean = jnp.mean(rows, axis=-1, keepdims=True)
    centered = rows - mean
    variance = jnp.mean(centered * centered, axis=-1, keepdims=True)
    inverse = lax.rsqrt(variance + EPS)
    return centered * inverse, inverse


def normalise_back(grad, unit, inverse, gain):
    scaled = grad * gain
    mean = jnp.mean(scaled, axis=-1, keepdims=True)
    along = jnp.mean(scaled * unit, axis=-1, keepdims=True)
    return inverse * (scaled - mean - unit * along)


def piece_starts(at, core, half):
    other = (1 - at) * half
    quarter = half // 2
    return (
        (pl.multiple_of(at * half, quarter), half),
        (pl.multiple_of(other + core * quarter, quarter), quarter),
        (pl.multiple_of(other + (1 - core) * quarter, quarter), quarter),
    )


def front_body(place, x_ref, mine_ref, theirs_ref, *rest):
    weights, (out_ref, h_ref, bias_ref) = rest[:9], rest[9:]
    at, core = place[0], place[1]
    step = pl.program_id(0)
    half = weights[0].shape[0]
    wide = weights[0].shape[1]

    @pl.when(step == 0)
    def _():
        unit, _ = normalise(x_ref[...].astype(F32))
        gain = full_row(at, mine_ref, theirs_ref, GAIN_ATTN)
        shift = full_row(at, mine_ref, theirs_ref, SHIFT_ATTN)
        h_ref[...] = (unit * gain + shift).astype(BF16)
        bias_ref[0:1, :] = full_row(at, mine_ref, theirs_ref, BIAS_QUERY)
        bias_ref[1:2, :] = jnp.zeros_like(bias_ref[1:2, :])
        bias_ref[2:3, :] = full_row(at, mine_ref, theirs_ref, BIAS_VALUE)

    starts = piece_starts(at, core, half)
    pieces = [h_ref[:, pl.ds(begin, size)] for begin, size in starts]
    columns = pl.ds(pl.multiple_of(step * wide, wide), wide)
    for part in range(3):
        total = bias_ref[part : part + 1, columns]
        for index in range(3):
            total = total + mm(pieces[index], weights[part * 3 + index][...])
        turned = total.T.astype(BF16)
        for head in range(wide // HEAD):
            out_ref[head, part] = turned[head * HEAD : (head + 1) * HEAD, :]


def front(place, x, mine, theirs, own, near, far):
    rows, width = x.shape
    heads = width // HEAD
    wide = 256
    steps = width // wide
    specs = []
    for part in range(3):
        for member in (own, near, far):
            specs.append(
                pl.BlockSpec(
                    (member.shape[0], wide), lambda i, _, part=part: (0, part * steps + i)
                )
            )
    return pl.pallas_call(
        front_body,
        grid_spec=pltpu.PrefetchScalarGridSpec(
            num_scalar_prefetch=1,
            grid=(steps,),
            in_specs=[whole(x.shape), whole(mine.shape), whole(theirs.shape)] + specs,
            out_specs=[
                pl.BlockSpec((wide // HEAD, 3, HEAD, rows), lambda i, _: (i, 0, 0, 0)),
                whole((rows, width)),
            ],
            scratch_shapes=[pltpu.VMEM((8, width), F32)],
        ),
        out_shape=[
            jax.ShapeDtypeStruct((heads, 3, HEAD, rows), BF16),
            jax.ShapeDtypeStruct((rows, width), BF16),
        ],
        compiler_params=params(),
        cost_estimate=cost(6 * rows * width * width, 6 * width * width + 10 * rows * width),
        name="front",
    )(place, x, mine, theirs, *([own, near, far] * 3))


def lay_out(source, target, part, per, tokens, sources, block, turned, scale):
    for src in range(sources):
        for pair in range(per):
            piece = source[src, part, :, pair * tokens : (pair + 1) * tokens]
            if scale is not None:
                piece = piece * jnp.asarray(scale, BF16)
            begin = src * tokens
            if turned:
                rows = piece.astype(F32).T.astype(BF16)
                target[pair, begin : begin + tokens, :] = rows
            else:
                inner = begin % block
                target[pair, begin // block, :, inner : inner + tokens] = piece


def attend_body(per, tokens, block, qkv_ref, out_ref, outf_ref, lse_ref, q_ref, k_ref, v_ref):
    sources = qkv_ref.shape[0]
    step = pl.program_id(0)

    @pl.when(step == 0)
    def _():
        lay_out(qkv_ref, q_ref, 0, per, tokens, sources, block, False, HEAD**-0.5)
        lay_out(qkv_ref, k_ref, 1, per, tokens, sources, block, True, None)
        lay_out(qkv_ref, v_ref, 2, per, tokens, sources, block, False, None)

    queries = [q_ref[pair, step] for pair in range(per)]

    def scores(pair, index):
        keys = k_ref[pair, pl.ds(pl.multiple_of(index * block, block), block), :]
        return mm(keys, queries[pair])

    key_at = lax.broadcasted_iota(jnp.int32, (block, block), 0)
    query_at = lax.broadcasted_iota(jnp.int32, (block, block), 1)
    carried = []
    for pair in range(per):
        masked = jnp.where(key_at <= query_at, scores(pair, step), LOWEST)
        top = jnp.max(masked, axis=0, keepdims=True)
        weights = jnp.exp(masked - top)
        total = jnp.sum(weights, axis=0, keepdims=True)
        mixed = mm(v_ref[pair, step], weights.astype(BF16))
        carried += [top, total, mixed]

    def one(index, state):
        fresh = []
        for pair in range(per):
            top, total, mixed = state[3 * pair : 3 * pair + 3]
            here = scores(pair, index)
            new_top = jnp.maximum(top, jnp.max(here, axis=0, keepdims=True))
            weights = jnp.exp(here - new_top)
            factor = jnp.exp(top - new_top)
            total = total * factor + jnp.sum(weights, axis=0, keepdims=True)
            mixed = mixed * factor + mm(v_ref[pair, index], weights.astype(BF16))
            fresh += [new_top, total, mixed]
        return tuple(fresh)

    final = lax.fori_loop(0, step, one, tuple(carried))
    for pair in range(per):
        top, total, mixed = final[3 * pair : 3 * pair + 3]
        mixed = mixed / total
        lse_ref[0, pair : pair + 1, :] = top + jnp.log(total)
        for dst in range(block // tokens):
            piece = mixed[:, dst * tokens : (dst + 1) * tokens]
            lanes = slice(pair * tokens, (pair + 1) * tokens)
            outf_ref[dst, :, lanes] = piece
            out_ref[dst, :, lanes] = piece.astype(BF16)


def attend(qkv, per):
    sources, _, _, lanes = qkv.shape
    tokens = lanes // per
    length = sources * tokens
    block = max(256, tokens)
    steps = length // block
    here = pl.BlockSpec((block // tokens, HEAD, lanes), lambda i: (i, 0, 0))
    return pl.pallas_call(
        functools.partial(attend_body, per, tokens, block),
        grid=(steps,),
        in_specs=[whole(qkv.shape)],
        out_specs=[here, here, pl.BlockSpec((1, 8, block), lambda i: (i, 0, 0))],
        out_shape=[
            jax.ShapeDtypeStruct((sources, HEAD, lanes), BF16),
            jax.ShapeDtypeStruct((sources, HEAD, lanes), F32),
            jax.ShapeDtypeStruct((steps, 8, block), F32),
        ],
        scratch_shapes=[
            pltpu.VMEM((per, steps, HEAD, block), BF16),
            pltpu.VMEM((per, length, HEAD), BF16),
            pltpu.VMEM((per, steps, HEAD, block), BF16),
        ],
        compiler_params=params(),
        cost_estimate=cost(
            8 * per * length * length * HEAD, 16 * qkv.size, per * length * length
        ),
        name="attend",
    )(qkv)


def attend_back_body(
    per, tokens, block, qkv_ref, go_ref, of_ref, lse_ref, out_ref, qt_ref, q_ref, kt_ref, k_ref, v_ref, g_ref,
    dk_ref, dv_ref,
):
    sources = qkv_ref.shape[0]
    step = pl.program_id(0)
    last = pl.num_programs(0) - 1

    @pl.when(step == 0)
    def _():
        lay_out(qkv_ref, qt_ref, 0, per, tokens, sources, block, False, HEAD**-0.5)
        lay_out(qkv_ref, q_ref, 0, per, tokens, sources, block, True, HEAD**-0.5)
        lay_out(qkv_ref, kt_ref, 1, per, tokens, sources, block, False, HEAD**-0.5)
        lay_out(qkv_ref, k_ref, 1, per, tokens, sources, block, True, None)
        lay_out(qkv_ref, v_ref, 2, per, tokens, sources, block, True, None)
        dk_ref[...] = jnp.zeros_like(dk_ref)
        dv_ref[...] = jnp.zeros_like(dv_ref)

    inner = block // tokens
    grads, deltas, lses, turned_grads, turned_queries, queries = [], [], [], [], [], []
    for pair in range(per):
        lanes = slice(pair * tokens, (pair + 1) * tokens)
        grad = jnp.concatenate([go_ref[dst, :, lanes] for dst in range(inner)], axis=1)
        mixed = jnp.concatenate([of_ref[dst, :, lanes] for dst in range(inner)], axis=1)
        wide = grad.astype(F32)
        grads.append(grad)
        deltas.append(jnp.sum(wide * mixed, axis=0, keepdims=True))
        turned_grads.append(wide.T.astype(BF16))
        lses.append(lse_ref[0, pair : pair + 1, :])
        queries.append(qt_ref[pair, step])
        turned_queries.append(q_ref[pair, pl.ds(pl.multiple_of(step * block, block), block), :])

    def one(index, state, diagonal):
        rows = pl.ds(pl.multiple_of(index * block, block), block)
        fresh = []
        for pair in range(per):
            weights = jnp.exp(mm(k_ref[pair, rows, :], queries[pair]) - lses[pair])
            if diagonal:
                key_at = lax.broadcasted_iota(jnp.int32, (block, block), 0)
                query_at = lax.broadcasted_iota(jnp.int32, (block, block), 1)
                weights = jnp.where(key_at <= query_at, weights, 0.0)
            back = mm(v_ref[pair, rows, :], grads[pair])
            dscore = (weights * (back - deltas[pair])).astype(BF16)
            dv_ref[pair, rows, :] += mm(weights.astype(BF16), turned_grads[pair])
            dk_ref[pair, rows, :] += mm(dscore, turned_queries[pair])
            fresh.append(state[pair] + mm(kt_ref[pair, index], dscore))
        return tuple(fresh)

    start = tuple(jnp.zeros((HEAD, block), F32) for _ in range(per))
    state = lax.fori_loop(0, step, lambda i, s: one(i, s, False), start)
    state = one(step, state, True)
    for pair in range(per):
        lanes = slice(pair * tokens, (pair + 1) * tokens)
        for dst in range(inner):
            out_ref[step * inner + dst, 0, :, lanes] = state[pair][
                :, dst * tokens : (dst + 1) * tokens
            ].astype(BF16)

    @pl.when(step == last)
    def _():
        for pair in range(per):
            lanes = slice(pair * tokens, (pair + 1) * tokens)
            for src in range(sources):
                rows = slice(src * tokens, (src + 1) * tokens)
                out_ref[src, 1, :, lanes] = dk_ref[pair, rows, :].T.astype(BF16)
                out_ref[src, 2, :, lanes] = dv_ref[pair, rows, :].T.astype(BF16)


def attend_back(qkv, grad, mixed, lse, per):
    sources, _, _, lanes = qkv.shape
    tokens = lanes // per
    length = sources * tokens
    block = max(256, tokens)
    steps = length // block
    here = pl.BlockSpec((block // tokens, HEAD, lanes), lambda i: (i, 0, 0))
    return pl.pallas_call(
        functools.partial(attend_back_body, per, tokens, block),
        grid=(steps,),
        in_specs=[whole(qkv.shape), here, here, pl.BlockSpec((1, 8, block), lambda i: (i, 0, 0))],
        out_specs=whole(qkv.shape),
        out_shape=jax.ShapeDtypeStruct(qkv.shape, BF16),
        scratch_shapes=[
            pltpu.VMEM((per, steps, HEAD, block), BF16),
            pltpu.VMEM((per, length, HEAD), BF16),
            pltpu.VMEM((per, steps, HEAD, block), BF16),
            pltpu.VMEM((per, length, HEAD), BF16),
            pltpu.VMEM((per, length, HEAD), BF16),
            pltpu.VMEM((8, 128), BF16),
            pltpu.VMEM((per, length, HEAD), F32),
            pltpu.VMEM((per, length, HEAD), F32),
        ],
        compiler_params=params(),
        cost_estimate=cost(
            20 * per * length * length * HEAD, 16 * qkv.size, per * length * length
        ),
        name="attend_back",
    )(qkv, grad, mixed, lse)


def middle_body(
    own_steps, place, x_ref, ot_ref, dy_ref, mine_ref, theirs_ref, mo_ref, mn_ref, mf_ref, eo_ref, en_ref, ef_ref,
    co_ref, cn_ref, cf_ref, out_ref, dx_ref, act_ref, du_ref, h_ref, da_ref, o_ref, dot_ref, sums_ref, be_ref,
    x1_ref, total_ref, dh_ref, bias_ref,
):
    at, core = place[0], place[1]
    step = pl.program_id(0)
    half = mo_ref.shape[0]
    starts = piece_starts(at, core, half)
    wide = act_ref.shape[1]
    near_steps = own_steps // 2
    block = expand_block(step, at, core, own_steps)

    @pl.when(step == 0)
    def _():
        mixed = ot_ref[...].astype(F32).T.astype(BF16)
        o_ref[...] = mixed
        merged = full_row(at, mine_ref, theirs_ref, BIAS_MERGE)
        for (begin, size), weight in zip(starts, (mo_ref, mn_ref, mf_ref)):
            merged = merged + mm(o_ref[:, pl.ds(begin, size)], weight[...])
        x1 = x_ref[...].astype(F32) + merged
        x1_ref[...] = x1
        unit, _ = normalise(x1)
        gain = full_row(at, mine_ref, theirs_ref, GAIN_MLP)
        shift = full_row(at, mine_ref, theirs_ref, SHIFT_MLP)
        h_ref[...] = (unit * gain + shift).astype(BF16)
        total_ref[...] = jnp.zeros_like(total_ref)
        dh_ref[...] = jnp.zeros_like(dh_ref)
        for row in range(own_steps):
            mine = mine_ref[BIAS_EXPAND + row : BIAS_EXPAND + row + 1, :].astype(F32)
            theirs = theirs_ref[BIAS_EXPAND + row : BIAS_EXPAND + row + 1, :].astype(F32)
            bias_ref[row : row + 1, :] = jnp.where(at == 0, mine, theirs)
            bias_ref[own_steps + row : own_steps + row + 1, :] = jnp.where(at == 0, theirs, mine)

    def work(contract):
        inner = bias_ref[pl.ds(block, 1), :]
        for (begin, size), weight in zip(starts, (eo_ref, en_ref, ef_ref)):
            inner = inner + mm(h_ref[:, pl.ds(begin, size)], weight[...])
        square = inner * inner
        bend = jnp.tanh(GELU_A * (inner + GELU_B * (inner * square)))
        active = (0.5 * inner * (1.0 + bend)).astype(BF16)
        slope = 0.5 * (1.0 + bend) + 0.5 * inner * (1.0 - bend * bend) * (
            GELU_A * (1.0 + 3.0 * GELU_B * square)
        )
        act_ref[...] = active
        total_ref[...] += mm(active, contract[...])
        grad = (mm_nt(dy_ref[...], contract[...]) * slope).astype(BF16)
        du_ref[...] = grad
        be_ref[pl.ds(block, 1), :] = jnp.sum(grad.astype(F32), axis=0, keepdims=True)
        for (begin, size), weight in zip(starts, (eo_ref, en_ref, ef_ref)):
            dh_ref[:, pl.ds(begin, size)] += mm_nt(grad, weight[...])

    @pl.when(step < own_steps)
    def _():
        work(co_ref)

    @pl.when(jnp.logical_and(step >= own_steps, step < own_steps + near_steps))
    def _():
        work(cn_ref)

    @pl.when(step >= own_steps + near_steps)
    def _():
        work(cf_ref)

    @pl.when(step == pl.num_programs(0) - 1)
    def _():
        x1 = x1_ref[...]
        bias = full_row(at, mine_ref, theirs_ref, BIAS_CONTRACT)
        out_ref[...] = (x1 + total_ref[...] + bias).astype(BF16)
        gain = full_row(at, mine_ref, theirs_ref, GAIN_MLP)
        unit, inverse = normalise(x1)
        grad = dh_ref[...]
        dy = dy_ref[...].astype(F32)
        dx = dy + normalise_back(grad, unit, inverse, gain)
        dx_ref[...] = dx
        da = dx.astype(BF16)
        da_ref[...] = da
        sums_ref[0:1, :] = jnp.sum(dy, axis=0, keepdims=True)
        sums_ref[1:2, :] = jnp.sum(grad * unit, axis=0, keepdims=True)
        sums_ref[2:3, :] = jnp.sum(grad, axis=0, keepdims=True)
        sums_ref[3:4, :] = jnp.sum(da.astype(F32), axis=0, keepdims=True)
        sums_ref[4:8, :] = jnp.zeros_like(sums_ref[4:8, :])
        for (begin, size), weight in zip(starts, (mo_ref, mn_ref, mf_ref)):
            dot_ref[pl.ds(begin, size), :] = mm_nt(weight[...], da).astype(BF16)


def expand_block(step, at, core, own_steps):
    near_steps = own_steps // 2
    other = (1 - at) * own_steps
    return jnp.where(
        step < own_steps,
        at * own_steps + step,
        jnp.where(
            step < own_steps + near_steps,
            other + core * near_steps + step - own_steps,
            other + (1 - core) * near_steps + step - own_steps - near_steps,
        ),
    )


def middle(place, x, ot, dy, mine, theirs, merge, expand, contract):
    rows, width = x.shape
    hidden = expand[0].shape[1]
    wide = 512
    own_steps = contract[0].shape[0] // wide
    near_steps = own_steps // 2
    steps = 2 * own_steps

    def column(i, place):
        return (0, expand_block(i, place[0], place[1], own_steps))

    def held(first, count):
        return lambda i, _: (jnp.clip(i - first, 0, count - 1), 0)

    in_specs = [whole(x.shape), whole(ot.shape), whole(dy.shape), whole(mine.shape), whole(theirs.shape)]
    in_specs += [whole(member.shape) for member in merge]
    in_specs += [pl.BlockSpec((member.shape[0], wide), column) for member in expand]
    in_specs += [
        pl.BlockSpec((wide, width), held(0, own_steps)),
        pl.BlockSpec((wide, width), held(own_steps, near_steps)),
        pl.BlockSpec((wide, width), held(own_steps + near_steps, near_steps)),
    ]
    shapes = [
        ((rows, width), BF16, None),
        ((rows, width), F32, None),
        ((rows, hidden), BF16, wide),
        ((rows, hidden), BF16, wide),
        ((rows, width), BF16, None),
        ((rows, width), BF16, None),
        ((rows, width), BF16, None),
        ((width, rows), BF16, None),
        ((8, width), F32, None),
        ((steps, wide), F32, None),
    ]
    return pl.pallas_call(
        functools.partial(middle_body, own_steps),
        grid_spec=pltpu.PrefetchScalarGridSpec(
            num_scalar_prefetch=1,
            grid=(steps,),
            in_specs=in_specs,
            out_specs=[
                whole(shape) if block is None else pl.BlockSpec((rows, block), column)
                for shape, _, block in shapes
            ],
            scratch_shapes=[
                pltpu.VMEM((rows, width), F32),
                pltpu.VMEM((rows, width), F32),
                pltpu.VMEM((rows, width), F32),
                pltpu.VMEM((steps, wide), F32),
            ],
        ),
        out_shape=[jax.ShapeDtypeStruct(shape, dtype) for shape, dtype, _ in shapes],
        compiler_params=params(),
        cost_estimate=cost(
            8 * rows * width * hidden + 4 * rows * width * width,
            4 * width * hidden + 2 * width * width + 30 * rows * width,
            rows * hidden,
        ),
        name="middle",
    )(place, x, ot, dy, mine, theirs, *merge, *expand, *contract)


def gram_body(aq, ax, ac, bq, bx, bc, out_ref):
    total = mm_tn(aq[...], bq[...])
    total = total + mm_tn(ax[...], bx[...])
    total = total + mm_tn(ac[0], bc[0])
    total = total + mm_tn(ac[1], bc[1])
    out_ref[0] = total.astype(BF16)


def gram(place, left, right, name):
    (aq, ax, ac), (bq, bx, bc) = left, right
    rows, columns = bq.shape
    quarter = ac.shape[2]
    high = min(quarter, 512)
    wide = 1024
    per = quarter // high
    return pl.pallas_call(
        lambda place, *refs: gram_body(*refs),
        grid_spec=pltpu.PrefetchScalarGridSpec(
            num_scalar_prefetch=1,
            grid=(columns // wide, per),
            in_specs=[
                pl.BlockSpec((rows, high), lambda j, i, s: (0, (s[0] * 2 + s[1]) * per + i)),
                pl.BlockSpec((rows, high), lambda j, i, s: (0, s[1] * per + i)),
                pl.BlockSpec((2, rows, high), lambda j, i, s: (0, 0, i)),
                pl.BlockSpec((rows, wide), lambda j, i, s: (0, j)),
                pl.BlockSpec((rows, wide), lambda j, i, s: (0, j)),
                pl.BlockSpec((2, rows, wide), lambda j, i, s: (0, 0, j)),
            ],
            out_specs=pl.BlockSpec((1, high, wide), lambda j, i, s: (j, i, 0)),
        ),
        out_shape=jax.ShapeDtypeStruct((columns // wide, quarter, wide), BF16),
        compiler_params=params(),
        cost_estimate=cost(
            8 * rows * quarter * columns, 8 * rows * (quarter + columns) + 2 * quarter * columns
        ),
        name=name,
    )(place, aq, ax, ac, bq, bx, bc)


def heads_body(dp_ref, h_ref, out_ref):
    @pl.when(pl.program_id(0) == 0)
    def _():
        out_ref[...] = jnp.zeros_like(out_ref)

    _, parts, head, lanes = dp_ref.shape
    out_ref[...] += mm(dp_ref[0].reshape(parts * head, lanes), h_ref[0])


def heads_gradient(dp, normed):
    sources, parts, head, lanes = dp.shape
    width = normed.shape[2]
    return pl.pallas_call(
        heads_body,
        grid=(sources,),
        in_specs=[
            pl.BlockSpec((1, parts, head, lanes), lambda i: (i, 0, 0, 0)),
            pl.BlockSpec((1, lanes, width), lambda i: (i, 0, 0)),
        ],
        out_specs=whole((parts * head, width)),
        out_shape=jax.ShapeDtypeStruct((parts * head, width), F32),
        compiler_params=params(),
        cost_estimate=cost(
            2 * sources * parts * head * lanes * width, 2 * sources * lanes * (width + parts * head)
        ),
        name="heads_gradient",
    )(dp, normed)


def spread_body(in_ref, out_ref):
    heads, _, head, half = in_ref.shape
    out_ref[...] = in_ref[...].reshape(heads * head, half).astype(F32).T


def spread_heads(gathered):
    heads, parts, head, half = gathered.shape
    some = 4
    steps = heads // some
    return pl.pallas_call(
        spread_body,
        grid=(parts, steps),
        in_specs=[pl.BlockSpec((some, 1, head, half), lambda t, i: (i, t, 0, 0))],
        out_specs=pl.BlockSpec((half, some * head), lambda t, i: (0, t * steps + i)),
        out_shape=jax.ShapeDtypeStruct((half, parts * heads * head), F32),
        compiler_params=params(),
        cost_estimate=cost(0, 6 * gathered.size),
        name="spread_heads",
    )(gathered)


def back_body(place, dp_ref, x_ref, dx_ref, mine_ref, theirs_ref, wo_ref, wn_ref, wf_ref, out_ref, sums_ref, dh_ref):
    at, core = place[0], place[1]
    part = pl.program_id(0)
    starts = piece_starts(at, core, wo_ref.shape[0])
    heads, _, head, rows = dp_ref.shape
    grad = dp_ref[...].reshape(heads * head, rows)

    @pl.when(part == 0)
    def _():
        dh_ref[...] = jnp.zeros_like(dh_ref)
        sums_ref[...] = jnp.zeros_like(sums_ref)

    for (begin, size), weight in zip(starts, (wo_ref, wn_ref, wf_ref)):
        dh_ref[pl.ds(begin, size), :] += mm(weight[...], grad)
    total = mm_nt(jnp.ones((8, rows), BF16), grad)

    @pl.when(part == 0)
    def _():
        sums_ref[2:3, :] = total[0:1, :]

    @pl.when(part == 2)
    def _():
        sums_ref[3:4, :] = total[0:1, :]
        dh = dh_ref[...].T
        unit, inverse = normalise(x_ref[...].astype(F32))
        gain = full_row(at, mine_ref, theirs_ref, GAIN_ATTN)
        out_ref[...] = dx_ref[...] + normalise_back(dh, unit, inverse, gain)
        sums_ref[0:1, :] = jnp.sum(dh * unit, axis=0, keepdims=True)
        sums_ref[1:2, :] = jnp.sum(dh, axis=0, keepdims=True)


def back(place, dp, x, dx, mine, theirs, weights):
    rows, width = x.shape
    heads, parts, head, _ = dp.shape
    return pl.pallas_call(
        back_body,
        grid_spec=pltpu.PrefetchScalarGridSpec(
            num_scalar_prefetch=1,
            grid=(parts,),
            in_specs=[
                pl.BlockSpec((heads, 1, head, rows), lambda t, _: (0, t, 0, 0)),
                whole(x.shape),
                whole(dx.shape),
                whole(mine.shape),
                whole(theirs.shape),
            ]
            + [pl.BlockSpec((member.shape[0], width), lambda t, _: (0, t)) for member in weights],
            out_specs=[whole((rows, width)), whole((8, width))],
            scratch_shapes=[pltpu.VMEM((width, rows), F32)],
        ),
        out_shape=[
            jax.ShapeDtypeStruct((rows, width), F32),
            jax.ShapeDtypeStruct((8, width), F32),
        ],
        compiler_params=params(),
        cost_estimate=cost(6 * rows * width * width, 6 * width * width + 14 * rows * width),
        name="back",
    )(place, dp, x, dx, mine, theirs, *weights)


def after(value, *others):
    return lax.optimization_barrier((value,) + others)[0]


def per_device(
    nctx, tokens_in, gain_attn, shift_attn, w_heads, bias_query, bias_value, w_merge, bias_merge, gain_mlp, shift_mlp,
    w_expand, bias_expand, w_contract, bias_contract, cotangent,
):
    seqs, tokens, width = tokens_in.shape
    rows = seqs * tokens
    half = width // 2
    heads = width // HEAD
    hidden = w_expand.shape[1]
    pairs = seqs * heads
    same = max(1, nctx // pairs)
    per = max(1, pairs // nctx)
    groups = seqs // per
    ctx = lax.axis_index("ctx")
    at = lax.axis_index("fsdp")
    core = ctx % 2
    place = jnp.stack([at, core]).astype(jnp.int32)
    chips = [[2 * chip + one for chip in range(nctx // 2)] for one in range(2)]

    def over_x(value):
        return lax.ppermute(value, "fsdp", [(0, 1), (1, 0)])

    def over_core(value):
        return lax.ppermute(value, "ctx", [(i, i ^ 1) for i in range(nctx)])

    def exchange(value):
        return lax.all_to_all(value, "ctx", 0, 0)

    def gather_weight(weight, *first):
        quarter = weight.shape[0] // 2
        mine = lax.dynamic_slice_in_dim(weight, core * quarter, quarter, 0)
        near = over_x(after(mine, *first))
        return weight, near, over_core(near)

    mine = jnp.concatenate(
        [
            member.reshape(-1, half)
            for member in (
                gain_attn, shift_attn, bias_query, bias_value, bias_merge, gain_mlp, shift_mlp, bias_contract,
                bias_expand, jnp.zeros(((-8 - bias_expand.shape[0] // half) % 16 * half,), BF16),
            )
        ]
    )
    theirs = over_x(mine)
    heads_w = gather_weight(w_heads)
    merge_w = gather_weight(w_merge, heads_w[1])
    expand_w = gather_weight(w_expand, heads_w[1])

    x = tokens_in.reshape(rows, width)
    dy = cotangent.reshape(rows, width)

    def to_send(value):
        lead = value.shape[1:-1]
        value = value.reshape((heads,) + lead + (groups, per * tokens))
        value = jnp.moveaxis(value, -2, 1).reshape((nctx // same,) + lead + (per * tokens,))
        return value if same == 1 else jnp.repeat(value, same, axis=0)

    def received(value):
        value = value[::same]
        lead = value.shape[1:-1]
        value = value.reshape((heads, groups) + lead + (per * tokens,))
        return jnp.moveaxis(value, 1, -2).reshape((heads,) + lead + (rows,))

    projected, normed = front(place, x, mine, theirs, *heads_w)
    normed_all = lax.all_gather(normed, "ctx", axis=0, tiled=False)
    qkv = exchange(to_send(projected))
    contract_w = gather_weight(w_contract, expand_w[1], qkv)
    mixed_b, mixed_f, lse = attend(qkv, per)
    mixed = received(exchange(mixed_b)).reshape(width, rows)
    block_out, dx1, active, du, normed_two, da, mixed_rows, grad_mixed, sums_mlp, sums_expand = middle(
        place, x, mixed, dy, mine, theirs, merge_w, expand_w, contract_w
    )

    def columns_of_four(value, first=()):
        two = value.shape[1] // 2
        one = two // 2
        there = over_x(after(lax.dynamic_slice_in_dim(value, (1 - at) * two, two, 1), *first))
        sent = jnp.stack(
            [
                lax.dynamic_slice_in_dim(value, at * two + (1 - core) * one, one, 1),
                lax.dynamic_slice_in_dim(there, (1 - core) * one, one, 1),
            ]
        )
        return value, there, over_core(sent)

    def tokens_of_four(value, *first):
        there = over_x(after(value, *first))
        return value, there, over_core(jnp.stack([value, there]))

    dy_four = tokens_of_four(dy, contract_w[1])
    grad_contract = gram(place, columns_of_four(active), dy_four, "grad_contract")
    grad_expand = gram(place, columns_of_four(normed_two), tokens_of_four(du), "grad_expand")
    grad_merge = gram(place, columns_of_four(mixed_rows), tokens_of_four(da), "grad_merge")

    grad_out = exchange(to_send(grad_mixed.reshape(heads, HEAD, rows)))
    dqkv = attend_back(qkv, grad_out, mixed_f, lse, per)
    dp = received(exchange(dqkv))

    def summed(value):
        part = lax.psum_scatter(
            value, "ctx", scatter_dimension=1, tiled=True, axis_index_groups=chips
        )
        whole_of = lax.all_gather(part, "ctx", axis=0, tiled=False)
        whole_of = whole_of.reshape((nctx // 2, 2) + part.shape)
        return jnp.transpose(whole_of, (1, 0, 3, 2, 4)).astype(F32)

    contract_sum = summed(grad_contract).reshape(w_contract.shape)
    others = summed(jnp.concatenate([grad_expand, grad_merge]))
    expand_sum = others[:, :, :, : hidden // width].reshape(w_expand.shape)
    merge_sum = others[:, :, :, hidden // width :].reshape(w_merge.shape)

    if groups > 1:
        normed_here = lax.dynamic_slice_in_dim(normed_all, (ctx // same % groups) * tokens * per, tokens * per, 1)
    else:
        normed_here = normed_all
    grad_heads = heads_gradient(dqkv, normed_here)
    if groups > 1:
        members = [
            [first + one + same * group for group in range(groups)]
            for first in range(0, nctx, groups * same)
            for one in range(same)
        ]
        grad_heads = lax.psum(grad_heads, "ctx", axis_index_groups=members)
    kept = lax.dynamic_slice_in_dim(grad_heads, at * half, half, 1)
    sent = lax.dynamic_slice_in_dim(grad_heads, (1 - at) * half, half, 1)
    kept = (kept + over_x(sent.astype(BF16)).astype(F32)).astype(BF16)
    spread = lax.all_gather(kept, "ctx", axis=0, tiled=False)[:: groups * same]
    heads_sum = spread_heads(spread.reshape(heads, 3, HEAD, half))

    grad_tokens, sums_attn = back(place, dp, x, dx1, mine, theirs, heads_w)

    vectors = jnp.concatenate(
        [
            jnp.concatenate([sums_mlp[:4], sums_attn[:4]]).reshape(8, 2, half),
            sums_expand.reshape(2, -1, half).swapaxes(0, 1),
        ]
    ).swapaxes(0, 1)
    mine_v = lax.dynamic_index_in_dim(vectors, at, 0, keepdims=False)
    vector = mine_v + over_x(lax.dynamic_index_in_dim(vectors, 1 - at, 0, keepdims=False))
    vector = jnp.sum(exchange(jnp.broadcast_to(vector, (nctx,) + vector.shape)), axis=0)
    return (
        block_out.reshape(tokens_in.shape),
        grad_tokens.reshape(tokens_in.shape),
        vector[4],
        vector[5],
        heads_sum,
        vector[6],
        vector[7],
        merge_sum,
        vector[3],
        vector[1],
        vector[2],
        expand_sum,
        vector[8:].reshape(-1),
        contract_sum,
        vector[0],
    )


def solution(mesh):
    rows, vec, mat = P("fsdp", "ctx", None), P("fsdp"), P("fsdp", None)
    return jax.shard_map(
        functools.partial(per_device, mesh.shape["ctx"]),
        mesh=mesh,
        in_specs=(rows, vec, vec, mat, vec, vec, mat, vec, vec, vec, mat, vec, mat, vec, rows),
        out_specs=(rows, rows, vec, vec, mat, vec, vec, mat, vec, vec, vec, mat, vec, mat, vec),
        check_vma=False,
    )
```

time: 1720 us -> 659 us (0.38)
  waiting for transfers between devices: 1210 us -> 340 us
  matrix products: 182 us -> 0 us
  blocking collectives: 205 us -> 60.2 us
  Pallas kernels: 0 us -> 128 us
  starting transfers between devices: 0.7 us -> 35.7 us
  local copies, waits for them, and re-layouts: 85.3 us -> 55.3 us
    all_gather x8 -> x4, waiting for transfers between devices: 409 us -> 0.03 us  [the longest x2 0.03 us: summed(): whole_of = lax.all_gather(part, 'ctx', axis=0, tiled=False)]
    reduce_scatter x4 -> x2, waiting for transfers between devices: 441 us -> 40.2 us  [summed(): lax.psum_scatter(value, 'ctx', scatter_dimension=1, tiled=True, axis_inde...]
    psum x1 -> x0, waiting for transfers between devices: 355 us -> none  [per_device(): lax.psum((halves[0], halves[1], halves[2], halves[3], halves[4], halves[5...]
    ppermute x0 -> x23, waiting for transfers between devices: none -> 247 us  [the longest x13 243 us: over_x(): return lax.ppermute(value, 'fsdp', [(0, 1), (1, 0)])]
    dot_general x28 -> x0, matrix products: 182 us -> none  [the longest x4 39 us: owner_compute(): jnp.einsum('shqk,sqhe->shke', dscore, q_piece, preferred_element_type=jnp...]
    all_gather x11 -> x0, blocking collectives: 135 us -> none  [the longest x1 75.7 us: per_device(): lax.all_gather(delta_rows, 'ctx', axis=1, tiled=True)]
    pallas_call x0 -> x10, Pallas kernels: none -> 128 us  [the longest x1 27 us: attend_back(): pl.pallas_call(functools.partial(attend_back_body, per, tokens, block), g...]
    psum x1 -> x0, blocking collectives: 62 us -> none  [per_device(): lax.psum((halves[0], halves[1], halves[2], halves[3], halves[4], halves[5...]
  transfers between devices with their start and end apart: 13 -> 32, of which waited for: 10 -> 17; matrix products, arithmetic and copies ran while one was open for 15% -> 4% of each run, Pallas kernels for 0% -> 14%
where the time goes in v1:
time: 659 us; the launch traced here: 651 us
  waiting for transfers between devices  340 us (52%)
  Pallas kernels  128 us (19%)
  blocking collectives  60.2 us (9%)
  local copies, waits for them, and re-layouts  55.3 us (8%)
  starting transfers between devices  35.7 us (5%)
  between operations  16.6 us (3%)
  other arithmetic  16.3 us (2%)
    ppermute x13, waiting for transfers between devices, over_x(): return lax.ppermute(value, 'fsdp', [(0, 1), (1, 0)])  243 us
    all_to_all x2, blocking collectives, exchange(): return lax.all_to_all(value, 'ctx', 0, 0)  60.2 us
    all_to_all x3, waiting for transfers between devices, exchange(): return lax.all_to_all(value, 'ctx', 0, 0)  52.2 us
    reduce_scatter x2, waiting for transfers between devices, summed(): lax.psum_scatter(value, 'ctx', scatter_dimension=1, tiled=True, axis_inde...  40.2 us
    pallas_call x1, Pallas kernels, attend_back(): pl.pallas_call(functools.partial(attend_back_body, per, tokens, block), g...  27 us
    pallas_call x1, Pallas kernels, attend(): pl.pallas_call(functools.partial(attend_body, per, tokens, block), grid=(...  26.5 us
    pallas_call x1, Pallas kernels, middle(): pl.pallas_call(functools.partial(middle_body, own_steps), grid_spec=pltpu...  22.9 us
    unnamed x59, local copies, waits for them, and re-layouts  20.7 us
  transfers between devices with their start and end apart: 32, of which 17 were waited for; matrix products, arithmetic and copies ran while one was open for 4% of the time, Pallas kernels for 14%

profile of v1, /device:TPU:0, one launch (start us, length us, event | category | flops | bytes accessed | tf_op | source)
XLA Modules:
  0.0 651.4 jit_solution(1722396086263489884)
XLA Ops:
  8.1 1.6 constant_dynamic-slice_fusion.6
  9.7 3.0 collective-permute-start.1
  12.7 34.4 %collective-permute-done.1.rest_1_.rest_4_.rest_7_.wn_ref = bf16[256,3072]{1,0:T(8,128)(2,1)S(1)} collective-permute-done((bf16[256,3072]{1,0:T(8,128)(2,1)S(1)}, bf16[256,3072]{1,0:T(8,128)(2,1)S(1)}, u32[]{:S(2)}, u32[]{:S(2)}) %collective-permute-start.1) | collective-permute-done | bytes 1572896 | tf_op jit(solution)/shard_map/ppermute | solution.py:676
  47.4 1.8 collective-permute-start
  49.3 1.9 collective-permute-done.theirs_ref
  51.2 6.9 %front.1 = (bf16[16,3,64,256]{3,2,1,0:T(8,128)(2,1)}, bf16[256,1024]{1,0:T(8,128)(2,1)}) custom-call(s32[2]{0:T(128)S(1)} %pad_add_fusion.place, bf16[256,1024]{1,0:T(8,128)(2,1)S(1)} %bitcast.61, bf16[16,512]{1,0:T(8,128)(2,1)S(1)} %concatenate.12.mine_ref, bf16[16,512]{1,0:T(8,128)(2,1)S(1)} %collective-permute-done.theirs_ref, bf16[512,3072]{1,0:T(8,128)(2,1)} %wo_ref.1, ...), custom_call_target="tpu_custom_call" | custom-call | flops 1610612736 | bytes 8912896 | tf_op jit(solution)/shard_map/front/pallas_call | solution.py:123
  58.1 6.2 all-to-all-start
  64.4 3.1 constant_dynamic-slice_fusion.4
  69.0 1.8 constant_dynamic-slice_fusion.3
  70.8 45.0 %collective-permute-done.5.en_ref = bf16[256,4096]{1,0:T(8,128)(2,1)} collective-permute-done((bf16[256,4096]{1,0:T(8,128)(2,1)}, bf16[256,4096]{1,0:T(8,128)(2,1)}, u32[]{:S(2)}, u32[]{:S(2)}) %collective-permute-start.5) | collective-permute-done | bytes 2097184 | tf_op jit(solution)/shard_map/ppermute | solution.py:676
  117.2 45.7 %collective-permute-done.7.cn_ref = bf16[1024,1024]{1,0:T(8,128)(2,1)} collective-permute-done((bf16[1024,1024]{1,0:T(8,128)(2,1)S(1)}, bf16[1024,1024]{1,0:T(8,128)(2,1)}, u32[]{:S(2)}, u32[]{:S(2)}) %collective-permute-start.7) | collective-permute-done | bytes 2097184 | tf_op jit(solution)/shard_map/ppermute | solution.py:676
  162.9 1.5 collective-permute-start.3
  164.5 26.5 %attend.1 = (bf16[16,64,256]{2,1,0:T(8,128)(2,1)}, f32[16,64,256]{2,1,0:T(8,128)S(1)}, f32[8,8,256]{2,1,0:T(8,128)S(1)}) custom-call(bf16[16,3,64,256]{3,2,1,0:T(8,128)(2,1)} %all-to-all-done.qkv_ref), custom_call_target="tpu_custom_call" | custom-call | flops 4294967296 | bytes 12582912 | tf_op jit(solution)/shard_map/attend/pallas_call | solution.py:219
  192.0 5.5 all-to-all-start.1
  198.6 1.5 collective-permute-done.4.mf_ref
  200.2 11.9 %all-to-all-done.1 = bf16[16,64,256]{2,1,0:T(8,128)(2,1)S(1)} async-done(((bf16[16,64,256]{2,1,0:T(8,128)(2,1)}), bf16[16,64,256]{2,1,0:T(8,128)(2,1)S(1)}, u32[]{:S(2)}, u32[]{:S(2)}) %all-to-all-start.1) | async-done | bytes 524320 | tf_op jit(solution)/shard_map/all_to_all | solution.py:682
  212.8 22.9 %middle.1 = (bf16[256,1024]{1,0:T(8,128)(2,1)}, f32[256,1024]{1,0:T(8,128)}, bf16[256,4096]{1,0:T(8,128)(2,1)}, bf16[256,4096]{1,0:T(8,128)(2,1)}, bf16[256,1024...) custom-call(s32[2]{0:T(128)S(1)} %pad_add_fusion.place, ...), custom_call_target="tpu_custom_call" | custom-call | flops 9663676416 | bytes 26738688 | tf_op jit(solution)/shard_map/middle/pallas_call | solution.py:475
  235.7 2.5 constant_dynamic-slice_fusion
  240.2 34.4 %collective-permute-done.21.refs_4_ = bf16[256,1024]{1,0:T(8,128)(2,1)S(1)} collective-permute-done((bf16[256,1024]{1,0:T(8,128)(2,1)S(1)}, bf16[256,1024]{1,0:T(8,128)(2,1)S(1)}, u32[]{:S(2)}, u32[]{:S(2)}) %collective-permute-start.21) | collective-permute-done | bytes 524320 | tf_op jit(solution)/shard_map/ppermute | solution.py:676
  277.7 2.3 collective-permute-done.20.refs_2_
  281.0 5.8 grad_contract.1
  288.1 47.5 %collective-permute-done.13.refs_4_ = bf16[256,4096]{1,0:T(8,128)(2,1)S(1)} collective-permute-done((bf16[256,4096]{1,0:T(8,128)(2,1)}, bf16[256,4096]{1,0:T(8,128)(2,1)S(1)}, u32[]{:S(2)}, u32[]{:S(2)}) %collective-permute-start.13) | collective-permute-done | bytes 2097184 | tf_op jit(solution)/shard_map/ppermute | solution.py:676
  335.6 4.8 pad_maximum_fusion
  340.9 13.8 %collective-permute-done.17.refs_4_ = bf16[256,1024]{1,0:T(8,128)(2,1)S(1)} collective-permute-done((bf16[256,1024]{1,0:T(8,128)(2,1)S(1)}, bf16[256,1024]{1,0:T(8,128)(2,1)S(1)}, u32[]{:S(2)}, u32[]{:S(2)}) %collective-permute-start.17) | collective-permute-done | bytes 524320 | tf_op jit(solution)/shard_map/ppermute | solution.py:676
  355.6 1.5 collective-permute-start.11
  357.2 6.9 %collective-permute-done.15.refs_1_ = bf16[256,512]{1,0:T(8,128)(2,1)S(1)} collective-permute-done((bf16[256,512]{1,0:T(8,128)(2,1)S(1)}, bf16[256,512]{1,0:T(8,128)(2,1)S(1)}, u32[]{:S(2)}, u32[]{:S(2)}) %collective-permute-start.15) | collective-permute-done | bytes 262176 | tf_op jit(solution)/shard_map/ppermute | solution.py:676
  364.2 5.1 collective-permute-done.11.refs_1_
  370.5 2.8 grad_merge.1
  373.3 7.1 %grad_expand.1 = bf16[4,256,1024]{2,1,0:T(8,128)(2,1)} custom-call(s32[2]{0:T(128)S(1)} %pad_add_fusion.place, bf16[256,1024]{1,0:T(8,128)(2,1)S(1)} %get-tuple-element.51.refs_0_, bf16[256,512]{1,0:T(8,128)(2,1)S(1)} %collective-permute-done.11.refs_1_, bf16[2,256,256]{2,1,0:T(8,128)(2,1)S(1)} %collective-permute-done.12.refs_2_, ...), custom_call_target="tpu_custom_call" | custom-call | flops 2147483648 | bytes 11010048 | tf_op jit(solution)/shard_map/grad_expand/pallas_call | solution.py:518
  380.4 3.3 pad_maximum_fusion.1
  383.8 5.1 reduce-scatter.5.cloned.1.call-done
  389.1 23.9 %all_to_all.25.go_ref = bf16[16,64,256]{2,1,0:T(8,128)(2,1)S(1)} all-to-all(bf16[16,64,256]{2,1,0:T(8,128)(2,1)S(1)} %bitcast.80), channel_id=1, replica_groups=mesh['ctx'=16,'fsdp'=2] {'ctx'}, dimensions={0} | all-to-all | bytes 1048576 | tf_op jit(solution)/shard_map/all_to_all | solution.py:682
  412.9 27.0 %attend_back.1.dp_ref = bf16[16,3,64,256]{3,2,1,0:T(8,128)(2,1)} custom-call(bf16[16,3,64,256]{3,2,1,0:T(8,128)(2,1)} %all-to-all-done.qkv_ref, bf16[16,64,256]{2,1,0:T(8,128)(2,1)S(1)} %all_to_all.25.go_ref, f32[16,64,256]{2,1,0:T(8,128)S(1)} %copy-done.6, f32[8,8,256]{2,1,0:T(8,128)S(1)} %get-tuple-element.44.lse_ref), custom_call_target="tpu_custom_call" | custom-call | flops 10737418240 | bytes 12582912 | tf_op jit(solution)/shard_map/attend_back/pallas_call | solution.py:317
  440.0 11.5 %heads_gradient.1 = f32[192,1024]{1,0:T(8,128)S(1)} custom-call(bf16[16,3,64,256]{3,2,1,0:T(8,128)(2,1)} %attend_back.1.dp_ref, bf16[16,256,1024]{2,1,0:T(8,128)(2,1)} %bitcast.70), custom_call_target="tpu_custom_call" | custom-call | flops 1610612736 | bytes 9961472 | tf_op jit(solution)/shard_map/heads_gradient/pallas_call | solution.py:554
  453.1 5.6 collective-permute-done.10
  459.4 35.0 %reduce-scatter.3.cloned.1.call-done = bf16[5,32,1024]{2,1,0:T(8,128)(2,1)} async-done(((bf16[5,256,1024]{2,1,0:T(8,128)(2,1)}), bf16[5,32,1024]{2,1,0:T(8,128)(2,1)}) %reduce-scatter.3.cloned.1.call-update) | async-done | bytes 327696 | tf_op jit(solution)/shard_map/reduce_scatter | solution.py:755
  494.5 4.1 all-to-all-start.3
  498.7 40.4 %all-to-all-done.3.dp_ref = bf16[16,3,64,256]{3,2,1,0:T(8,128)(2,1)S(1)} async-done(((bf16[16,3,64,256]{3,2,1,0:T(8,128)(2,1)}), bf16[16,3,64,256]{3,2,1,0:T(8,128)(2,1)S(1)}, u32[]{:S(2)}, u32[]{:S(2)}) %all-to-all-start.3) | async-done | bytes 1572896 | tf_op jit(solution)/shard_map/all_to_all | solution.py:682
  540.2 7.7 %back.1 = (f32[256,1024]{1,0:T(8,128)}, f32[8,1024]{1,0:T(8,128)S(1)}) custom-call(s32[2]{0:T(128)S(1)} %pad_add_fusion.place, bf16[16,3,64,256]{3,2,1,0:T(8,128)(2,1)} %copy-done.9, bf16[256,1024]{1,0:T(8,128)(2,1)S(1)} %bitcast.62, f32[256,1024]{1,0:T(8,128)S(1)} %copy-done.4, bf16[16,512]{1,0:T(8,128)(2,1)S(1)} %concatenate.12.mine_ref, ...), custom_call_target="tpu_custom_call" | custom-call | flops 1610612736 | bytes 9961472 | tf_op jit(solution)/shard_map/back/pallas_call | solution.py:626
  549.4 2.4 collective-permute-done.9
  551.9 36.4 %all_to_all.26 = f32[16,12,512]{2,1,0:T(8,128)S(1)} all-to-all(f32[16,12,512]{2,1,0:T(8,128)S(1)} %broadcast_in_dim.3), channel_id=1, replica_groups=mesh['ctx'=16,'fsdp'=2] {'ctx'}, dimensions={0} | all-to-all | bytes 786432 | tf_op jit(solution)/shard_map/all_to_all | solution.py:682
  589.6 3.2 convert_bitcast_fusion.1
  592.8 4.2 copy.42
  597.0 9.2 %spread_heads.1 = f32[512,3072]{1,0:T(8,128)} custom-call(bf16[16,3,64,512]{3,2,1,0:T(8,128)(2,1)} %bitcast.77), custom_call_target="tpu_custom_call" | custom-call | bytes 9437184 | tf_op jit(solution)/shard_map/spread_heads/pallas_call | solution.py:580
  606.3 3.8 convert_bitcast_fusion
  610.4 4.2 slice.60
  616.1 12.3 %copy.41 = f32[2,8,32,4,1024]{4,3,2,1,0:T(4,128)} copy(f32[2,8,32,4,1024]{4,2,3,0,1:T(8,128)} %slice.60) | data formatting | bytes 16777216 | tf_op jit(solution)/shard_map/slice | solution.py:764
  628.4 15.1 %copy.53 = f32[64,8,4,1024]{3,1,2,0:T(8,128)} copy(f32[64,8,4,1024]{3,2,1,0:T(4,128)} %bitcast.69) | data formatting | bytes 16777216
  (143 shorter events, 24.2 us)
Async XLA Ops:
  8.0 39.1 %copy-start.18 = (bf16[512]{0:T(512)(128)(2,1)S(1)}, bf16[512]{0:T(512)(128)(2,1)}, u32[]{:S(2)}) copy-start(bf16[512]{0:T(512)(128)(2,1)} %param.16) | copy-start | bytes 3076
  8.0 39.1 %copy-start.19 = (bf16[512]{0:T(512)(128)(2,1)S(1)}, bf16[512]{0:T(512)(128)(2,1)}, u32[]{:S(2)}) copy-start(bf16[512]{0:T(512)(128)(2,1)} %param.17) | copy-start | bytes 3076
  8.0 39.1 %copy-start.20 = (bf16[512]{0:T(512)(128)(2,1)S(1)}, bf16[512]{0:T(512)(128)(2,1)}, u32[]{:S(2)}) copy-start(bf16[512]{0:T(512)(128)(2,1)} %param.19) | copy-start | bytes 3076
  8.0 39.1 %copy-start.21 = (bf16[512]{0:T(512)(128)(2,1)S(1)}, bf16[512]{0:T(512)(128)(2,1)}, u32[]{:S(2)}) copy-start(bf16[512]{0:T(512)(128)(2,1)} %param.20) | copy-start | bytes 3076
  8.1 39.2 %copy-start.22 = (bf16[512]{0:T(512)(128)(2,1)S(1)}, bf16[512]{0:T(512)(128)(2,1)}, u32[]{:S(2)}) copy-start(bf16[512]{0:T(512)(128)(2,1)} %param.22) | copy-start | bytes 3076
  8.1 39.2 %copy-start.23 = (bf16[512]{0:T(512)(128)(2,1)S(1)}, bf16[512]{0:T(512)(128)(2,1)}, u32[]{:S(2)}) copy-start(bf16[512]{0:T(512)(128)(2,1)} %param.23) | copy-start | bytes 3076
  8.1 39.2 %copy-start.24 = (bf16[512]{0:T(512)(128)(2,1)S(1)}, bf16[512]{0:T(512)(128)(2,1)}, u32[]{:S(2)}) copy-start(bf16[512]{0:T(512)(128)(2,1)} %param.24) | copy-start | bytes 3076
  8.1 39.2 %copy-start.25 = (bf16[512]{0:T(512)(128)(2,1)S(1)}, bf16[512]{0:T(512)(128)(2,1)}, u32[]{:S(2)}) copy-start(bf16[512]{0:T(512)(128)(2,1)} %param.28) | copy-start | bytes 3076
  8.1 39.2 %copy-start.17 = (bf16[2048]{0:T(1024)(128)(2,1)S(1)}, bf16[2048]{0:T(1024)(128)(2,1)}, u32[]{:S(2)}) copy-start(bf16[2048]{0:T(1024)(128)(2,1)} %param.26) | copy-start | bytes 12292
  8.1 43.1 %copy-start = (bf16[2,128,1024]{2,1,0:T(8,128)(2,1)S(1)}, bf16[2,128,1024]{2,1,0:T(8,128)(2,1)}, u32[]{:S(2)}) copy-start(bf16[2,128,1024]{2,1,0:T(8,128)(2,1)} %param.15) | copy-start | bytes 1572868
  9.7 37.4 %collective-permute-start.1 = (bf16[256,3072]{1,0:T(8,128)(2,1)S(1)}, bf16[256,3072]{1,0:T(8,128)(2,1)S(1)}, u32[]{:S(2)}, u32[]{:S(2)}) collective-permute-start(bf16[256,3072]{1,0:T(8,128)(2,1)S(1)} %constant_dynamic-slice_fusion.6), channel_id=1, source_target_pairs={{0,1},{1,0},{2,3},{3,2},{4,5},{5,4},{6,7},{7,6},{8,9},{9,8},{10,11... | collective-permute-start | bytes 4718600 | tf_op jit(solution)/shard_map/ppermute | solution.py:676
  47.1 4.1 collective-permute-start.2
  47.4 3.8 collective-permute-start
  58.1 57.6 %all-to-all-start = ((bf16[16,3,64,256]{3,2,1,0:T(8,128)(2,1)}), bf16[16,3,64,256]{3,2,1,0:T(8,128)(2,1)}, u32[]{:S(2)}, u32[]{:S(2)}) async-start(bf16[16,3,64,256]{3,2,1,0:T(8,128)(2,1)} %get-tuple-element.36), calls=%async_computation | async-start | bytes 3145728 | tf_op jit(solution)/shard_map/all_to_all | solution.py:682
  67.5 95.4 %copy-start.16 = (bf16[512,1024]{1,0:T(8,128)(2,1)S(1)}, bf16[512,1024]{1,0:T(8,128)(2,1)}, u32[]{:S(2)}) copy-start(bf16[512,1024]{1,0:T(8,128)(2,1)} %mo_ref.1) | copy-start | bytes 3145732
  67.5 48.2 %collective-permute-start.5 = (bf16[256,4096]{1,0:T(8,128)(2,1)}, bf16[256,4096]{1,0:T(8,128)(2,1)}, u32[]{:S(2)}, u32[]{:S(2)}) collective-permute-start(bf16[256,4096]{1,0:T(8,128)(2,1)} %constant_dynamic-slice_fusion.4), channel_id=1, source_target_pairs={{0,1},{1,0},{2,3},{3,2},{4,5},{5,4},{6,7},{7,6},{8,9},{9,8},{10,11... | collective-permute-start | bytes 6291464 | tf_op jit(solution)/shard_map/ppermute | solution.py:676
  115.7 47.2 %collective-permute-start.7 = (bf16[1024,1024]{1,0:T(8,128)(2,1)S(1)}, bf16[1024,1024]{1,0:T(8,128)(2,1)}, u32[]{:S(2)}, u32[]{:S(2)}) collective-permute-start(bf16[1024,1024]{1,0:T(8,128)(2,1)S(1)} %constant_dynamic-slice_fusion.3), channel_id=1, source_target_pairs={{0,1},{1,0},{2,3},{3,2},{4,5},{5,4},{6,7},{7,6},{8,9},{9,8},{10,11... | collective-permute-start | bytes 6291464 | tf_op jit(solution)/shard_map/ppermute | solution.py:676
  117.2 83.0 %collective-permute-start.6 = (bf16[256,4096]{1,0:T(8,128)(2,1)}, bf16[256,4096]{1,0:T(8,128)(2,1)}, u32[]{:S(2)}, u32[]{:S(2)}) collective-permute-start(bf16[256,4096]{1,0:T(8,128)(2,1)} %collective-permute-done.5.en_ref), channel_id=1, source_target_pairs={{0,2},{2,0},{4,6},{6,4},{8,10},{10,8},{12,14},{14,12},{16,18},{18,... | collective-permute-start | bytes 6291464 | tf_op jit(solution)/shard_map/ppermute | solution.py:679
  162.9 49.1 %collective-permute-start.8 = (bf16[1024,1024]{1,0:T(8,128)(2,1)}, bf16[1024,1024]{1,0:T(8,128)(2,1)}, u32[]{:S(2)}, u32[]{:S(2)}) collective-permute-start(bf16[1024,1024]{1,0:T(8,128)(2,1)} %collective-permute-done.7.cn_ref), channel_id=1, source_target_pairs={{0,2},{2,0},{4,6},{6,4},{8,10},{10,8},{12,14},{14,12},{16,18},{18,... | collective-permute-start | bytes 6291464 | tf_op jit(solution)/shard_map/ppermute | solution.py:679
  162.9 35.2 %collective-permute-start.3 = (bf16[256,1024]{1,0:T(8,128)(2,1)S(1)}, bf16[256,1024]{1,0:T(8,128)(2,1)S(1)}, u32[]{:S(2)}, u32[]{:S(2)}) collective-permute-start(bf16[256,1024]{1,0:T(8,128)(2,1)S(1)} %constant_dynamic-slice_fusion.5), channel_id=1, source_target_pairs={{0,1},{1,0},{2,3},{3,2},{4,5},{5,4},{6,7},{7,6},{8,9},{9,8},{10,11... | collective-permute-start | bytes 1572872 | tf_op jit(solution)/shard_map/ppermute | solution.py:676
  192.0 20.0 %all-to-all-start.1 = ((bf16[16,64,256]{2,1,0:T(8,128)(2,1)}), bf16[16,64,256]{2,1,0:T(8,128)(2,1)S(1)}, u32[]{:S(2)}, u32[]{:S(2)}) async-start(bf16[16,64,256]{2,1,0:T(8,128)(2,1)} %get-tuple-element.37), calls=%async_computation.1 | async-start | bytes 1048576 | tf_op jit(solution)/shard_map/all_to_all | solution.py:682
  197.6 191.4 %reduce-scatter.5.cloned.1.call-start = ((), (), s32[]{:S(2)}) async-start(), calls=%async_computation.8 | async-start | bytes 2359296 | tf_op jit(solution)/shard_map/reduce_scatter | solution.py:755
  198.2 2.0 collective-permute-start.4
  212.8 25.9 %copy-start.2 = (bf16[2,128,1024]{2,1,0:T(8,128)(2,1)S(1)}, bf16[2,128,1024]{2,1,0:T(8,128)(2,1)}, u32[]{:S(2)}) copy-start(bf16[2,128,1024]{2,1,0:T(8,128)(2,1)} %param.29) | copy-start | bytes 1572868
  235.7 119.0 %copy-start.3 = (bf16[256,1024]{1,0:T(8,128)(2,1)}, bf16[256,1024]{1,0:T(8,128)(2,1)S(1)}, u32[]{:S(2)}) copy-start(bf16[256,1024]{1,0:T(8,128)(2,1)S(1)} %get-tuple-element.54.refs_3_) | copy-start | bytes 1572868
  238.2 37.7 %collective-permute-start.19 = (bf16[256,2048]{1,0:T(8,128)(2,1)}, bf16[256,2048]{1,0:T(8,128)(2,1)}, u32[]{:S(2)}, u32[]{:S(2)}) collective-permute-start(bf16[256,2048]{1,0:T(8,128)(2,1)} %constant_dynamic-slice_fusion), channel_id=1, source_target_pairs={{0,1},{1,0},{2,3},{3,2},{4,5},{5,4},{6,7},{7,6},{8,9},{9,8},{10,11... | collective-permute-start | bytes 3145736 | tf_op jit(solution)/shard_map/ppermute | solution.py:676
  238.7 35.9 %collective-permute-start.21 = (bf16[256,1024]{1,0:T(8,128)(2,1)S(1)}, bf16[256,1024]{1,0:T(8,128)(2,1)S(1)}, u32[]{:S(2)}, u32[]{:S(2)}) collective-permute-start(bf16[256,1024]{1,0:T(8,128)(2,1)S(1)} %bitcast.64), channel_id=1, source_target_pairs={{0,1},{1,0},{2,3},{3,2},{4,5},{5,4},{6,7},{7,6},{8,9},{9,8},{10,11... | collective-permute-start | bytes 1572872 | tf_op jit(solution)/shard_map/ppermute | solution.py:676
  274.8 2.9 collective-permute-start.22
  277.1 2.8 collective-permute-start.20
  286.8 153.2 %all-gather.9.cloned.1.call-start = ((), (), s32[]{:S(2)}) async-start(), calls=%async_computation.9 | async-start | bytes 8912896 | tf_op jit(solution)/shard_map/all_gather | solution.py:720
  287.4 207.1 %reduce-scatter.3.cloned.1.call-start = ((), (), s32[]{:S(2)}) async-start(), calls=%async_computation.7 | async-start | bytes 2949120 | tf_op jit(solution)/shard_map/reduce_scatter | solution.py:755
  287.4 48.2 %collective-permute-start.13 = (bf16[256,4096]{1,0:T(8,128)(2,1)}, bf16[256,4096]{1,0:T(8,128)(2,1)S(1)}, u32[]{:S(2)}, u32[]{:S(2)}) collective-permute-start(bf16[256,4096]{1,0:T(8,128)(2,1)} %get-tuple-element.52.refs_3_), channel_id=1, source_target_pairs={{0,1},{1,0},{2,3},{3,2},{4,5},{5,4},{6,7},{7,6},{8,9},{9,8},{10,11... | collective-permute-start | bytes 6291464 | tf_op jit(solution)/shard_map/ppermute | solution.py:676
  340.4 32.9 %collective-permute-start.14 = (bf16[2,256,4096]{2,1,0:T(8,128)(2,1)}, bf16[2,256,4096]{2,1,0:T(8,128)(2,1)}, u32[]{:S(2)}, u32[]{:S(2)}) collective-permute-start(bf16[2,256,4096]{2,1,0:T(8,128)(2,1)} %pad_maximum_fusion), channel_id=1, source_target_pairs={{0,2},{2,0},{4,6},{6,4},{8,10},{10,8},{12,14},{14,12},{16,18},{18,... | collective-permute-start | bytes 12582920 | tf_op jit(solution)/shard_map/ppermute | solution.py:679
  340.4 14.3 %collective-permute-start.17 = (bf16[256,1024]{1,0:T(8,128)(2,1)S(1)}, bf16[256,1024]{1,0:T(8,128)(2,1)S(1)}, u32[]{:S(2)}, u32[]{:S(2)}) collective-permute-start(bf16[256,1024]{1,0:T(8,128)(2,1)S(1)} %get-tuple-element.54.refs_3_), channel_id=1, source_target_pairs={{0,1},{1,0},{2,3},{3,2},{4,5},{5,4},{6,7},{7,6},{8,9},{9,8},{10,11... | collective-permute-start | bytes 1572872 | tf_op jit(solution)/shard_map/ppermute | solution.py:676
  354.8 14.6 %collective-permute-start.18 = (bf16[2,256,1024]{2,1,0:T(8,128)(2,1)S(1)}, bf16[2,256,1024]{2,1,0:T(8,128)(2,1)S(1)}, u32[]{:S(2)}, u32[]{:S(2)}) collective-permute-start(bf16[2,256,1024]{2,1,0:T(8,128)(2,1)S(1)} %pad_maximum_fusion.2), channel_id=1, source_target_pairs={{0,2},{2,0},{4,6},{6,4},{8,10},{10,8},{12,14},{14,12},{16,18},{18,... | collective-permute-start | bytes 3145736 | tf_op jit(solution)/shard_map/ppermute | solution.py:679
  354.9 9.2 %collective-permute-start.15 = (bf16[256,512]{1,0:T(8,128)(2,1)S(1)}, bf16[256,512]{1,0:T(8,128)(2,1)S(1)}, u32[]{:S(2)}, u32[]{:S(2)}) collective-permute-start(bf16[256,512]{1,0:T(8,128)(2,1)S(1)} %constant_dynamic-slice_fusion.1), channel_id=1, source_target_pairs={{0,1},{1,0},{2,3},{3,2},{4,5},{5,4},{6,7},{7,6},{8,9},{9,8},{10,11... | collective-permute-start | bytes 786440 | tf_op jit(solution)/shard_map/ppermute | solution.py:676
  355.6 13.7 %collective-permute-start.11 = (bf16[256,512]{1,0:T(8,128)(2,1)S(1)}, bf16[256,512]{1,0:T(8,128)(2,1)S(1)}, u32[]{:S(2)}, u32[]{:S(2)}) collective-permute-start(bf16[256,512]{1,0:T(8,128)(2,1)S(1)} %constant_dynamic-slice_fusion.2), channel_id=1, source_target_pairs={{0,1},{1,0},{2,3},{3,2},{4,5},{5,4},{6,7},{7,6},{8,9},{9,8},{10,11... | collective-permute-start | bytes 786440 | tf_op jit(solution)/shard_map/ppermute | solution.py:676
  364.2 5.3 collective-permute-start.16
  369.4 3.9 collective-permute-start.12
  383.8 29.2 %copy-start.6 = (f32[16,64,256]{2,1,0:T(8,128)S(1)}, f32[16,64,256]{2,1,0:T(8,128)}, u32[]{:S(2)}) copy-start(f32[16,64,256]{2,1,0:T(8,128)} %copy-done.5) | copy-start | bytes 3145732
  383.8 205.8 %all-gather.15.cloned.1.call-start = ((), (), s32[]{:S(2)}) async-start(), calls=%async_computation.12 | async-start | bytes 4456448 | tf_op jit(solution)/shard_map/all_gather | solution.py:758
  389.0 208.0 %all-gather.11.cloned.1.call-start = ((), (), s32[]{:S(2)}) async-start(), calls=%async_computation.10 | async-start | bytes 3342336 | tf_op jit(solution)/shard_map/all_gather | solution.py:782
  451.5 88.7 %copy-start.1 = (bf16[2,128,1024]{2,1,0:T(8,128)(2,1)S(1)}, bf16[2,128,1024]{2,1,0:T(8,128)(2,1)}, u32[]{:S(2)}) copy-start(bf16[2,128,1024]{2,1,0:T(8,128)(2,1)} %param.15) | copy-start | bytes 1572868
  451.5 88.7 %copy-start.4 = (f32[256,1024]{1,0:T(8,128)S(1)}, f32[256,1024]{1,0:T(8,128)}, u32[]{:S(2)}) copy-start(f32[256,1024]{1,0:T(8,128)} %get-tuple-element.45.dx_ref) | copy-start | bytes 3145732
  451.6 7.1 %collective-permute-start.10 = (bf16[192,512]{1,0:T(8,128)(2,1)S(1)}, bf16[192,512]{1,0:T(8,128)(2,1)S(1)}, u32[]{:S(2)}, u32[]{:S(2)}) collective-permute-start(bf16[192,512]{1,0:T(8,128)(2,1)S(1)} %dynamic-slice_convert_fusion), channel_id=1, source_target_pairs={{0,1},{1,0},{2,3},{3,2},{4,5},{5,4},{6,7},{7,6},{8,9},{9,8},{10,11... | collective-permute-start | bytes 589832 | tf_op jit(solution)/shard_map/ppermute | solution.py:676
  459.4 146.9 %all-gather.13.cloned.1.call-start = ((), (), s32[]{:S(2)}) async-start(), calls=%async_computation.11 | async-start | bytes 5570560 | tf_op jit(solution)/shard_map/all_gather | solution.py:758
  494.5 44.6 %all-to-all-start.3 = ((bf16[16,3,64,256]{3,2,1,0:T(8,128)(2,1)}), bf16[16,3,64,256]{3,2,1,0:T(8,128)(2,1)S(1)}, u32[]{:S(2)}, u32[]{:S(2)}) async-start(bf16[16,3,64,256]{3,2,1,0:T(8,128)(2,1)} %attend_back.1.dp_ref), calls=%async_computation.3 | async-start | bytes 3145728 | tf_op jit(solution)/shard_map/all_to_all | solution.py:682
  547.9 4.0 collective-permute-start.9
  (12 other events, 61.7 us)
Sparse Core Ops, SparseCore 0:
  286.9 102.0 reduce-scatter.4
  393.1 101.3 reduce-scatter.2
Sparse Core Ops, SparseCore 1:
  289.4 80.1 all-gather.8
  389.1 67.4 all-gather.14
  459.5 65.4 all-gather.10
  527.3 70.2 all-gather.12

commit v2 on v1

v2 whole, which is shorter than its diff:
```python
import functools
import math

import jax
import jax.numpy as jnp
from jax import lax
from jax.experimental import pallas as pl
from jax.experimental.pallas import tpu as pltpu
from jax.sharding import PartitionSpec as P

HEAD = 64
EPS = 1e-05
LOWEST = -1e30
GELU_A = math.sqrt(2.0 / math.pi)
GELU_B = 0.044715
F32 = jnp.float32
BF16 = jnp.bfloat16
VMEM_BYTES = 52 * 1024 * 1024
GAIN_ATTN, SHIFT_ATTN, BIAS_QUERY, BIAS_VALUE = 0, 1, 2, 3
BIAS_MERGE, GAIN_MLP, SHIFT_MLP, BIAS_CONTRACT = 4, 5, 6, 7
BIAS_EXPAND = 8


def mm(left, right):
    return jnp.dot(left, right, preferred_element_type=F32)


def mm_nt(left, right):
    return lax.dot_general(left, right, (((1,), (1,)), ((), ())), preferred_element_type=F32)


def mm_tn(left, right):
    return lax.dot_general(left, right, (((0,), (0,)), ((), ())), preferred_element_type=F32)


def params(**extra):
    return pltpu.CompilerParams(vmem_limit_bytes=VMEM_BYTES, **extra)


def about(us):
    return pl.CostEstimate(flops=int(us * 1.15e9), bytes_accessed=0, transcendentals=0)


def whole(shape):
    return pl.BlockSpec(shape, lambda *_: (0,) * len(shape))


def full_row(at, mine_ref, theirs_ref, row):
    mine = mine_ref[row : row + 1, :].astype(F32)
    theirs = theirs_ref[row : row + 1, :].astype(F32)
    low = jnp.where(at == 0, mine, theirs)
    high = jnp.where(at == 0, theirs, mine)
    return jnp.concatenate([low, high], axis=1)


def normalise(rows):
    mean = jnp.mean(rows, axis=-1, keepdims=True)
    centered = rows - mean
    variance = jnp.mean(centered * centered, axis=-1, keepdims=True)
    inverse = lax.rsqrt(variance + EPS)
    return centered * inverse, inverse


def normalise_back(grad, unit, inverse, gain):
    scaled = grad * gain
    mean = jnp.mean(scaled, axis=-1, keepdims=True)
    along = jnp.mean(scaled * unit, axis=-1, keepdims=True)
    return inverse * (scaled - mean - unit * along)


def piece_starts(at, core, half):
    other = (1 - at) * half
    quarter = half // 2
    return (
        (pl.multiple_of(at * half, quarter), half),
        (pl.multiple_of(other + core * quarter, quarter), quarter),
        (pl.multiple_of(other + (1 - core) * quarter, quarter), quarter),
    )


def project(at, core, normed, bias, own, near, far, out_ref, part):
    total = bias
    for (begin, size), weight in zip(piece_starts(at, core, own.shape[0]), (own, near, far)):
        total = total + mm(normed[:, pl.ds(begin, size)], weight[...])
    turned = total.T.astype(BF16)
    for head in range(turned.shape[0] // HEAD):
        piece = turned[head * HEAD : (head + 1) * HEAD, :]
        if part is None:
            out_ref[head] = piece
        else:
            out_ref[head, part] = piece


def front_query_body(place, x_ref, mine_ref, theirs_ref, own, near, far, out_ref, h_ref, bias_ref):
    at, core = place[0], place[1]
    step = pl.program_id(0)
    wide = own.shape[1]

    @pl.when(step == 0)
    def _():
        unit, _ = normalise(x_ref[...].astype(F32))
        gain = full_row(at, mine_ref, theirs_ref, GAIN_ATTN)
        shift = full_row(at, mine_ref, theirs_ref, SHIFT_ATTN)
        h_ref[...] = (unit * gain + shift).astype(BF16)
        bias_ref[0:1, :] = full_row(at, mine_ref, theirs_ref, BIAS_QUERY)

    columns = pl.ds(pl.multiple_of(step * wide, wide), wide)
    project(at, core, h_ref, bias_ref[0:1, columns], own, near, far, out_ref, None)


def front_query(place, x, mine, theirs, own, near, far):
    rows, width = x.shape
    heads = width // HEAD
    wide = 256
    return pl.pallas_call(
        front_query_body,
        grid_spec=pltpu.PrefetchScalarGridSpec(
            num_scalar_prefetch=1,
            grid=(width // wide,),
            in_specs=[whole(x.shape), whole(mine.shape), whole(theirs.shape)]
            + [pl.BlockSpec((member.shape[0], wide), lambda i, _: (0, i)) for member in (own, near, far)],
            out_specs=[
                pl.BlockSpec((wide // HEAD, HEAD, rows), lambda i, _: (i, 0, 0)),
                whole((rows, width)),
            ],
            scratch_shapes=[pltpu.VMEM((8, width), F32)],
        ),
        out_shape=[
            jax.ShapeDtypeStruct((heads, HEAD, rows), BF16),
            jax.ShapeDtypeStruct((rows, width), BF16),
        ],
        compiler_params=params(),
        cost_estimate=about(4),
        name="front_query",
    )(place, x, mine, theirs, own, near, far)


def front_rest_body(place, h_ref, mine_ref, theirs_ref, *rest):
    weights, (out_ref, bias_ref) = rest[:6], rest[6:]
    at, core = place[0], place[1]
    step = pl.program_id(0)
    wide = weights[0].shape[1]

    @pl.when(step == 0)
    def _():
        bias_ref[0:1, :] = jnp.zeros_like(bias_ref[0:1, :])
        bias_ref[1:2, :] = full_row(at, mine_ref, theirs_ref, BIAS_VALUE)

    columns = pl.ds(pl.multiple_of(step * wide, wide), wide)
    for part in range(2):
        bias = bias_ref[part : part + 1, columns]
        project(at, core, h_ref, bias, *weights[3 * part : 3 * part + 3], out_ref, part)


def front_rest(place, normed, mine, theirs, own, near, far):
    rows, width = normed.shape
    heads = width // HEAD
    wide = 256
    steps = width // wide
    specs = []
    for part in range(2):
        for member, skip in ((own, 1), (near, 0), (far, 0)):
            first = (part + skip) * steps
            specs.append(pl.BlockSpec((member.shape[0], wide), lambda i, _, first=first: (0, first + i)))
    return pl.pallas_call(
        front_rest_body,
        grid_spec=pltpu.PrefetchScalarGridSpec(
            num_scalar_prefetch=1,
            grid=(steps,),
            in_specs=[whole(normed.shape), whole(mine.shape), whole(theirs.shape)] + specs,
            out_specs=pl.BlockSpec((wide // HEAD, 2, HEAD, rows), lambda i, _: (i, 0, 0, 0)),
            scratch_shapes=[pltpu.VMEM((8, width), F32)],
        ),
        out_shape=jax.ShapeDtypeStruct((heads, 2, HEAD, rows), BF16),
        compiler_params=params(),
        cost_estimate=about(5),
        name="front_rest",
    )(place, normed, mine, theirs, *([own, near, far] * 2))


def lay_out(source, target, per, tokens, block, turned=False, scale=None):
    for src in range(source.shape[0]):
        for pair in range(per):
            piece = source[src, :, pair * tokens : (pair + 1) * tokens]
            if scale is not None:
                piece = piece * jnp.asarray(scale, BF16)
            begin = src * tokens
            if turned:
                target[pair, begin : begin + tokens, :] = piece.astype(F32).T.astype(BF16)
            else:
                inner = begin % block
                target[pair, begin // block, :, inner : inner + tokens] = piece


def allowed_at(first_key, first_query, keys, queries):
    key_at = first_key + lax.broadcasted_iota(jnp.int32, (keys, queries), 0)
    query_at = first_query + lax.broadcasted_iota(jnp.int32, (keys, queries), 1)
    return key_at <= query_at


def attend_body(per, tokens, block, chunk, query_ref, kv_ref, out_ref, outf_ref, lse_ref, q_ref, k_ref, v_ref):
    step = pl.program_id(0)

    @pl.when(step == 0)
    def _():
        lay_out(query_ref, q_ref, per, tokens, block, scale=HEAD**-0.5)
        lay_out(kv_ref.at[:, 0], k_ref, per, tokens, chunk, turned=True)
        lay_out(kv_ref.at[:, 1], v_ref, per, tokens, chunk)

    queries = [q_ref[pair, step] for pair in range(per)]

    def scores(pair, index):
        keys = k_ref[pair, pl.ds(pl.multiple_of(index * chunk, chunk), chunk), :]
        return mm(keys, queries[pair])

    last = (step * block) // chunk
    allowed = allowed_at(last * chunk, step * block, chunk, block)
    carried = []
    for pair in range(per):
        masked = jnp.where(allowed, scores(pair, last), LOWEST)
        top = jnp.max(masked, axis=0, keepdims=True)
        weights = jnp.exp(masked - top)
        total = jnp.sum(weights, axis=0, keepdims=True)
        mixed = mm(v_ref[pair, last], weights.astype(BF16))
        carried += [top, total, mixed]

    def one(index, state):
        fresh = []
        for pair in range(per):
            top, total, mixed = state[3 * pair : 3 * pair + 3]
            here = scores(pair, index)
            new_top = jnp.maximum(top, jnp.max(here, axis=0, keepdims=True))
            weights = jnp.exp(here - new_top)
            factor = jnp.exp(top - new_top)
            total = total * factor + jnp.sum(weights, axis=0, keepdims=True)
            mixed = mixed * factor + mm(v_ref[pair, index], weights.astype(BF16))
            fresh += [new_top, total, mixed]
        return tuple(fresh)

    final = lax.fori_loop(0, last, one, tuple(carried))
    for pair in range(per):
        top, total, mixed = final[3 * pair : 3 * pair + 3]
        mixed = mixed / total
        lse_ref[0, pair : pair + 1, :] = top + jnp.log(total)
        for dst in range(block // tokens):
            piece = mixed[:, dst * tokens : (dst + 1) * tokens]
            lanes = slice(pair * tokens, (pair + 1) * tokens)
            outf_ref[dst, :, lanes] = piece
            out_ref[dst, :, lanes] = piece.astype(BF16)


def attend(query, kv, per, block=512, chunk=512):
    sources, _, lanes = query.shape
    tokens = lanes // per
    length = sources * tokens
    steps = length // block
    here = pl.BlockSpec((block // tokens, HEAD, lanes), lambda i: (i, 0, 0))
    return pl.pallas_call(
        functools.partial(attend_body, per, tokens, block, chunk),
        grid=(steps,),
        in_specs=[whole(query.shape), whole(kv.shape)],
        out_specs=[here, here, pl.BlockSpec((1, 8, block), lambda i: (i, 0, 0))],
        out_shape=[
            jax.ShapeDtypeStruct((sources, HEAD, lanes), BF16),
            jax.ShapeDtypeStruct((sources, HEAD, lanes), F32),
            jax.ShapeDtypeStruct((steps, 8, block), F32),
        ],
        scratch_shapes=[
            pltpu.VMEM((per, steps, HEAD, block), BF16),
            pltpu.VMEM((per, length, HEAD), BF16),
            pltpu.VMEM((per, length // chunk, HEAD, chunk), BF16),
        ],
        compiler_params=params(),
        cost_estimate=about(20),
        name="attend",
    )(query, kv)


def attend_back_body(
    per, tokens, block, chunk, query_ref, kv_ref, go_ref, of_ref, lse_ref, out_ref, qt_ref, q_ref, kt_ref, k_ref, v_ref,
    dk_ref, dv_ref,
):
    sources = query_ref.shape[0]
    step = pl.program_id(0)

    @pl.when(step == 0)
    def _():
        lay_out(query_ref, qt_ref, per, tokens, block, scale=HEAD**-0.5)
        lay_out(query_ref, q_ref, per, tokens, block, turned=True, scale=HEAD**-0.5)
        lay_out(kv_ref.at[:, 0], kt_ref, per, tokens, chunk, scale=HEAD**-0.5)
        lay_out(kv_ref.at[:, 0], k_ref, per, tokens, chunk, turned=True)
        lay_out(kv_ref.at[:, 1], v_ref, per, tokens, chunk, turned=True)
        dk_ref[...] = jnp.zeros_like(dk_ref)
        dv_ref[...] = jnp.zeros_like(dv_ref)

    inner = block // tokens
    grads, deltas, lses, turned_grads, turned_queries, queries = [], [], [], [], [], []
    for pair in range(per):
        lanes = slice(pair * tokens, (pair + 1) * tokens)
        grad = jnp.concatenate([go_ref[dst, :, lanes] for dst in range(inner)], axis=1)
        mixed = jnp.concatenate([of_ref[dst, :, lanes] for dst in range(inner)], axis=1)
        wide = grad.astype(F32)
        grads.append(grad)
        deltas.append(jnp.sum(wide * mixed, axis=0, keepdims=True))
        turned_grads.append(wide.T.astype(BF16))
        lses.append(lse_ref[0, pair : pair + 1, :])
        queries.append(qt_ref[pair, step])
        turned_queries.append(q_ref[pair, pl.ds(pl.multiple_of(step * block, block), block), :])

    def one(index, state, allowed):
        rows = pl.ds(pl.multiple_of(index * chunk, chunk), chunk)
        fresh = []
        for pair in range(per):
            weights = jnp.exp(mm(k_ref[pair, rows, :], queries[pair]) - lses[pair])
            if allowed is not None:
                weights = jnp.where(allowed, weights, 0.0)
            back = mm(v_ref[pair, rows, :], grads[pair])
            dscore = (weights * (back - deltas[pair])).astype(BF16)
            dv_ref[pair, rows, :] += mm(weights.astype(BF16), turned_grads[pair])
            dk_ref[pair, rows, :] += mm(dscore, turned_queries[pair])
            fresh.append(state[pair] + mm(kt_ref[pair, index], dscore))
        return tuple(fresh)

    last = (step * block) // chunk
    start = tuple(jnp.zeros((HEAD, block), F32) for _ in range(per))
    state = lax.fori_loop(0, last, lambda i, s: one(i, s, None), start)
    state = one(last, state, allowed_at(last * chunk, step * block, chunk, block))
    for pair in range(per):
        lanes = slice(pair * tokens, (pair + 1) * tokens)
        for dst in range(inner):
            out_ref[step * inner + dst, 0, :, lanes] = state[pair][
                :, dst * tokens : (dst + 1) * tokens
            ].astype(BF16)

    @pl.when(step == pl.num_programs(0) - 1)
    def _():
        for pair in range(per):
            lanes = slice(pair * tokens, (pair + 1) * tokens)
            for src in range(sources):
                rows = slice(src * tokens, (src + 1) * tokens)
                out_ref[src, 1, :, lanes] = dk_ref[pair, rows, :].T.astype(BF16)
                out_ref[src, 2, :, lanes] = dv_ref[pair, rows, :].T.astype(BF16)


def attend_back(query, kv, grad, mixed, lse, per, chunk=512):
    sources, _, lanes = query.shape
    tokens = lanes // per
    length = sources * tokens
    steps, _, block = lse.shape
    here = pl.BlockSpec((block // tokens, HEAD, lanes), lambda i: (i, 0, 0))
    shape = (sources, 3, HEAD, lanes)
    return pl.pallas_call(
        functools.partial(attend_back_body, per, tokens, block, chunk),
        grid=(steps,),
        in_specs=[
            whole(query.shape), whole(kv.shape), here, here, pl.BlockSpec((1, 8, block), lambda i: (i, 0, 0)),
        ],
        out_specs=whole(shape),
        out_shape=jax.ShapeDtypeStruct(shape, BF16),
        scratch_shapes=[
            pltpu.VMEM((per, steps, HEAD, block), BF16),
            pltpu.VMEM((per, length, HEAD), BF16),
            pltpu.VMEM((per, length // chunk, HEAD, chunk), BF16),
            pltpu.VMEM((per, length, HEAD), BF16),
            pltpu.VMEM((per, length, HEAD), BF16),
            pltpu.VMEM((per, length, HEAD), F32),
            pltpu.VMEM((per, length, HEAD), F32),
        ],
        compiler_params=params(),
        cost_estimate=about(25),
        name="attend_back",
    )(query, kv, grad, mixed, lse)


def merge_body(place, x_ref, ot_ref, mine_ref, theirs_ref, mo_ref, mn_ref, mf_ref, x1_ref, h_ref, o_ref):
    at, core = place[0], place[1]
    starts = piece_starts(at, core, mo_ref.shape[0])
    o_ref[...] = ot_ref[...].astype(F32).T.astype(BF16)
    merged = full_row(at, mine_ref, theirs_ref, BIAS_MERGE)
    for (begin, size), weight in zip(starts, (mo_ref, mn_ref, mf_ref)):
        merged = merged + mm(o_ref[:, pl.ds(begin, size)], weight[...])
    x1 = x_ref[...].astype(F32) + merged
    x1_ref[...] = x1
    unit, _ = normalise(x1)
    gain = full_row(at, mine_ref, theirs_ref, GAIN_MLP)
    shift = full_row(at, mine_ref, theirs_ref, SHIFT_MLP)
    h_ref[...] = (unit * gain + shift).astype(BF16)


def merge(place, x, ot, mine, theirs, weights):
    shape = x.shape
    operands = (x, ot, mine, theirs, *weights)
    return pl.pallas_call(
        merge_body,
        grid_spec=pltpu.PrefetchScalarGridSpec(
            num_scalar_prefetch=1,
            grid=(1,),
            in_specs=[whole(member.shape) for member in operands],
            out_specs=[whole(shape)] * 3,
        ),
        out_shape=[
            jax.ShapeDtypeStruct(shape, F32),
            jax.ShapeDtypeStruct(shape, BF16),
            jax.ShapeDtypeStruct(shape, BF16),
        ],
        compiler_params=params(),
        cost_estimate=about(5),
        name="merge",
    )(place, *operands)


def gelu_pair(inner):
    square = inner * inner
    bend = jnp.tanh(GELU_A * (inner + GELU_B * (inner * square)))
    active = 0.5 * inner * (1.0 + bend)
    slope = 0.5 * (1.0 + bend) + 0.5 * inner * (1.0 - bend * bend) * (GELU_A * (1.0 + 3.0 * GELU_B * square))
    return active, slope


def read_expand_bias(at, mine_ref, theirs_ref, bias_ref):
    count = bias_ref.shape[0] // 2
    for row in range(count):
        mine = mine_ref[BIAS_EXPAND + row : BIAS_EXPAND + row + 1, :].astype(F32)
        theirs = theirs_ref[BIAS_EXPAND + row : BIAS_EXPAND + row + 1, :].astype(F32)
        bias_ref[row : row + 1, :] = jnp.where(at == 0, mine, theirs)
        bias_ref[count + row : count + row + 1, :] = jnp.where(at == 0, theirs, mine)


def mlp_body(
    own_steps, place, x1_ref, h_ref, dy_ref, mine_ref, theirs_ref, mo_ref, mn_ref, mf_ref, eo_ref, en_ref, ef_ref,
    co_ref, cr_ref, out_ref, dx_ref, da_ref, dot_ref, sums_ref, be_ref, total_ref, dh_ref, bias_ref,
):
    at, core = place[0], place[1]
    step = pl.program_id(0)
    starts = piece_starts(at, core, mo_ref.shape[0])
    block = hidden_block(step, at, own_steps)

    @pl.when(step == 0)
    def _():
        total_ref[...] = jnp.zeros_like(total_ref)
        dh_ref[...] = jnp.zeros_like(dh_ref)
        read_expand_bias(at, mine_ref, theirs_ref, bias_ref)

    def work(contract_ref):
        contract = contract_ref[...].reshape(-1, contract_ref.shape[-1])
        inner = bias_ref[pl.ds(block, 1), :]
        for (begin, size), weight in zip(starts, (eo_ref, en_ref, ef_ref)):
            inner = inner + mm(h_ref[:, pl.ds(begin, size)], weight[...])
        active, slope = gelu_pair(inner)
        total_ref[...] += mm(active.astype(BF16), contract)
        grad = (mm_nt(dy_ref[...], contract) * slope).astype(BF16)
        be_ref[pl.ds(block, 1), :] = jnp.sum(grad.astype(F32), axis=0, keepdims=True)
        for (begin, size), weight in zip(starts, (eo_ref, en_ref, ef_ref)):
            dh_ref[:, pl.ds(begin, size)] += mm_nt(grad, weight[...])

    @pl.when(step < own_steps)
    def _():
        work(co_ref)

    @pl.when(step >= own_steps)
    def _():
        work(cr_ref)

    @pl.when(step == pl.num_programs(0) - 1)
    def _():
        x1 = x1_ref[...]
        bias = full_row(at, mine_ref, theirs_ref, BIAS_CONTRACT)
        out_ref[...] = (x1 + total_ref[...] + bias).astype(BF16)
        gain = full_row(at, mine_ref, theirs_ref, GAIN_MLP)
        unit, inverse = normalise(x1)
        grad = dh_ref[...]
        dy = dy_ref[...].astype(F32)
        dx = dy + normalise_back(grad, unit, inverse, gain)
        dx_ref[...] = dx
        da = dx.astype(BF16)
        da_ref[...] = da
        sums_ref[0:1, :] = jnp.sum(dy, axis=0, keepdims=True)
        sums_ref[1:2, :] = jnp.sum(grad * unit, axis=0, keepdims=True)
        sums_ref[2:3, :] = jnp.sum(grad, axis=0, keepdims=True)
        sums_ref[3:4, :] = jnp.sum(da.astype(F32), axis=0, keepdims=True)
        sums_ref[4:8, :] = jnp.zeros_like(sums_ref[4:8, :])
        for (begin, size), weight in zip(starts, (mo_ref, mn_ref, mf_ref)):
            dot_ref[pl.ds(begin, size), :] = mm_nt(weight[...], da).astype(BF16)


def hidden_block(step, at, own_steps):
    return jnp.where(step < own_steps, at * own_steps + step, (1 - at) * own_steps + step - own_steps)


def mlp(place, x1, normed, dy, mine, theirs, merge_w, expand, contract, contract_rest):
    rows, width = x1.shape
    wide = 512
    own_steps = contract.shape[0] // wide
    shards = wide // contract_rest.shape[1]
    steps = 2 * own_steps
    operands = (x1, normed, dy, mine, theirs, *merge_w)
    in_specs = [whole(member.shape) for member in operands]
    in_specs += [
        pl.BlockSpec((member.shape[0], wide), lambda i, s: (0, hidden_block(i, s[0], own_steps)))
        for member in expand
    ]
    in_specs += [
        pl.BlockSpec((wide, width), lambda i, _: (jnp.minimum(i, own_steps - 1), 0)),
        pl.BlockSpec(
            (shards, contract_rest.shape[1], width), lambda i, _: (jnp.maximum(i - own_steps, 0), 0, 0)
        ),
    ]
    shapes = [
        ((rows, width), BF16),
        ((rows, width), F32),
        ((rows, width), BF16),
        ((width, rows), BF16),
        ((8, width), F32),
        ((steps, wide), F32),
    ]
    return pl.pallas_call(
        functools.partial(mlp_body, own_steps),
        grid_spec=pltpu.PrefetchScalarGridSpec(
            num_scalar_prefetch=1,
            grid=(steps,),
            in_specs=in_specs,
            out_specs=[whole(shape) for shape, _ in shapes],
            scratch_shapes=[
                pltpu.VMEM((rows, width), F32),
                pltpu.VMEM((rows, width), F32),
                pltpu.VMEM((steps, wide), F32),
            ],
        ),
        out_shape=[jax.ShapeDtypeStruct(shape, dtype) for shape, dtype in shapes],
        compiler_params=params(),
        cost_estimate=about(18),
        name="mlp",
    )(place, *operands, *expand, contract, contract_rest)


def hidden_part(step, at, core, own_steps):
    part = own_steps // 2
    return jnp.where(
        step < part, at * own_steps + core * part + step, (1 - at) * own_steps + core * part + step - part
    )


def weights_body(own_steps, place, *refs):
    h_refs, dy_refs = refs[:4], refs[4:8]
    mine_ref, theirs_ref, eo_ref, en_ref, ef_ref, co_ref, cr_ref, out_ref, bias_ref, contract_ref, expand_ref = refs[8:]
    at, core = place[0], place[1]
    step = pl.program_id(0)
    part = own_steps // 2
    half = eo_ref.shape[0]
    starts = piece_starts(at, core, half)
    block = hidden_part(step, at, core, own_steps)
    wide = eo_ref.shape[1]
    chips, _, width = out_ref.shape
    contract_rows = part * wide // chips
    expand_rows = half // chips

    @pl.when(step == 0)
    def _():
        read_expand_bias(at, mine_ref, theirs_ref, bias_ref)

    def work(weight_ref, forward):
        contract = weight_ref[...].reshape(wide, width)
        bias = bias_ref[pl.ds(block, 1), :]
        for index, (h_ref, dy_ref) in enumerate(zip(h_refs, dy_refs)):
            inner = bias
            for (begin, size), weight in zip(starts, (eo_ref, en_ref, ef_ref)):
                inner = inner + mm(h_ref[:, pl.ds(begin, size)], weight[...])
            active, slope = gelu_pair(inner)
            grad = (mm_nt(dy_ref[...], contract) * slope).astype(BF16)
            own = mm_tn(h_ref[:, pl.ds(pl.multiple_of(at * half, half), half)], grad)
            if index == 0:
                expand_ref[...] = own
            else:
                expand_ref[...] += own
            if forward:
                own = mm_tn(active.astype(BF16), dy_ref[...])
                if index == 0:
                    contract_ref[...] = own
                else:
                    contract_ref[...] += own

    def store_expand(column):
        for turn in range(2):
            place_of = jnp.where(turn == 0, at, 1 - at)
            rows = pl.ds(pl.multiple_of(contract_rows + place_of * expand_rows, expand_rows), expand_rows)

            @pl.when(step // part == turn)
            def _():
                for chip in range(chips):
                    out_ref[chip, rows, column * wide : (column + 1) * wide] = expand_ref[
                        chip * expand_rows : (chip + 1) * expand_rows, :
                    ].astype(BF16)

    for now in range(part):

        @pl.when(step == now)
        def _():
            work(co_ref, True)
            some = wide // contract_rows
            for chip in range(some):
                out_ref[now * some + chip, :contract_rows, :] = contract_ref[
                    chip * contract_rows : (chip + 1) * contract_rows, :
                ].astype(BF16)

    @pl.when(step >= part)
    def _():
        work(cr_ref, False)

    for column in range(part):

        @pl.when(step % part == column)
        def _():
            store_expand(column)


def mlp_weights(place, chips, normed, dy, mine, theirs, expand, contract, contract_rest):
    rows, width = dy[0].shape
    wide = 512
    half = expand[0].shape[0]
    own_steps = contract.shape[0] // wide
    part = own_steps // 2
    shards = wide // contract_rest.shape[1]
    operands = (*normed, *dy, mine, theirs)
    in_specs = [whole(member.shape) for member in operands]
    in_specs += [
        pl.BlockSpec((member.shape[0], wide), lambda i, s: (0, hidden_part(i, s[0], s[1], own_steps)))
        for member in expand
    ]
    in_specs += [
        pl.BlockSpec((wide, width), lambda i, s: (s[1] * part + jnp.minimum(i, part - 1), 0)),
        pl.BlockSpec(
            (shards, contract_rest.shape[1], width),
            lambda i, s: (s[1] * part + jnp.maximum(i - part, 0), 0, 0),
        ),
    ]
    shape = (chips, part * wide // chips + 2 * (half // chips), width)
    return pl.pallas_call(
        functools.partial(weights_body, own_steps),
        grid_spec=pltpu.PrefetchScalarGridSpec(
            num_scalar_prefetch=1,
            grid=(own_steps,),
            in_specs=in_specs,
            out_specs=whole(shape),
            scratch_shapes=[
                pltpu.VMEM((2 * own_steps, wide), F32),
                pltpu.VMEM((wide, width), F32),
                pltpu.VMEM((half, wide), F32),
            ],
        ),
        out_shape=jax.ShapeDtypeStruct(shape, BF16),
        compiler_params=params(),
        cost_estimate=about(20),
        name="mlp_weights",
    )(place, *operands, *expand, contract, contract_rest)


def spread_mlp_body(in_ref, contract_ref, expand_ref):
    _, _, contract_rows, width = contract_ref.shape
    expand_rows = expand_ref.shape[0]
    for core in range(2):
        contract_ref[core, 0] = in_ref[core, :contract_rows, :].astype(F32)
        for part in range(2):
            first = contract_rows + part * expand_rows
            begin = (2 * part + core) * width
            expand_ref[:, begin : begin + width] = in_ref[core, first : first + expand_rows, :].astype(F32)


def spread_mlp(gathered, contract_shape, expand_shape):
    devices, rows, width = gathered.shape
    chips = devices // 2
    contract_rows = contract_shape[0] // devices
    expand_rows = expand_shape[0] // chips
    contract, expand = pl.pallas_call(
        spread_mlp_body,
        grid=(chips,),
        in_specs=[pl.BlockSpec((2, rows, width), lambda i: (i, 0, 0))],
        out_specs=[
            pl.BlockSpec((2, 1, contract_rows, width), lambda i: (0, i, 0, 0)),
            pl.BlockSpec((expand_rows, expand_shape[1]), lambda i: (i, 0)),
        ],
        out_shape=[
            jax.ShapeDtypeStruct((2, chips, contract_rows, width), F32),
            jax.ShapeDtypeStruct(expand_shape, F32),
        ],
        compiler_params=params(),
        cost_estimate=about(8),
        name="spread_mlp",
    )(gathered)
    return contract.reshape(contract_shape), expand


def merge_weights_body(place, oo_ref, ox_ref, ao_ref, ax_ref, out_ref):
    out_ref[...] = (mm_tn(oo_ref[...], ao_ref[...]) + mm_tn(ox_ref[...], ax_ref[...])).astype(BF16)


def merge_weights(place, mixed, grad):
    rows, width = mixed[0].shape
    half = width // 2
    return pl.pallas_call(
        merge_weights_body,
        grid_spec=pltpu.PrefetchScalarGridSpec(
            num_scalar_prefetch=1,
            grid=(1,),
            in_specs=[pl.BlockSpec((rows, half), lambda i, s: (0, s[0]))] * 2 + [whole((rows, width))] * 2,
            out_specs=whole((half, width)),
        ),
        out_shape=jax.ShapeDtypeStruct((half, width), BF16),
        compiler_params=params(),
        cost_estimate=about(4),
        name="merge_weights",
    )(place, *mixed, *grad)


def heads_body(dp_ref, h_ref, out_ref):
    @pl.when(pl.program_id(0) == 0)
    def _():
        out_ref[...] = jnp.zeros_like(out_ref)

    _, parts, head, lanes = dp_ref.shape
    out_ref[...] += mm(dp_ref[0].reshape(parts * head, lanes), h_ref[0])


def heads_gradient(dp, normed):
    sources, parts, head, lanes = dp.shape
    width = normed.shape[2]
    return pl.pallas_call(
        heads_body,
        grid=(sources,),
        in_specs=[
            pl.BlockSpec((1, parts, head, lanes), lambda i: (i, 0, 0, 0)),
            pl.BlockSpec((1, lanes, width), lambda i: (i, 0, 0)),
        ],
        out_specs=whole((parts * head, width)),
        out_shape=jax.ShapeDtypeStruct((parts * head, width), F32),
        compiler_params=params(),
        cost_estimate=about(11),
        name="heads_gradient",
    )(dp, normed)


def spread_body(in_ref, heads_ref, merge_ref):
    heads, rows, half = in_ref.shape
    parts = heads_ref.shape[1] // (heads * HEAD)
    some = 4
    for part in range(parts):
        for first in range(0, heads, some):
            piece = in_ref[first : first + some, part * HEAD : (part + 1) * HEAD, :]
            column = (part * heads + first) * HEAD
            heads_ref[:, column : column + some * HEAD] = piece.reshape(some * HEAD, half).astype(F32).T
    merge_rows = merge_ref.shape[0] // heads
    for head in range(heads):
        for side in range(2):
            first = parts * HEAD + side * merge_rows
            merge_ref[head * merge_rows : (head + 1) * merge_rows, side * half : (side + 1) * half] = in_ref[
                head, first : first + merge_rows, :
            ].astype(F32)


def spread_heads(gathered, heads_shape, merge_shape):
    return pl.pallas_call(
        spread_body,
        out_shape=[jax.ShapeDtypeStruct(heads_shape, F32), jax.ShapeDtypeStruct(merge_shape, F32)],
        compiler_params=params(),
        cost_estimate=about(9),
        name="spread_heads",
    )(gathered)


def back_body(
    place, dp_ref, x_ref, dx_ref, mine_ref, theirs_ref, own_ref, qn_ref, qf_ref, rn_ref, rf_ref, out_ref, sums_ref, dh_ref
):
    at, core = place[0], place[1]
    part = pl.program_id(0)
    starts = piece_starts(at, core, own_ref.shape[0])
    heads, _, head, rows = dp_ref.shape

    @pl.when(part == 0)
    def _():
        dh_ref[...] = jnp.zeros_like(dh_ref)
        sums_ref[...] = jnp.zeros_like(sums_ref)

    def work(weights):
        grad = dp_ref[...].reshape(heads * head, rows)
        for (begin, size), weight in zip(starts, weights):
            dh_ref[pl.ds(begin, size), :] += mm(weight[...], grad)
        return mm_nt(jnp.ones((8, rows), BF16), grad)[0:1, :]

    @pl.when(part == 0)
    def _():
        sums_ref[2:3, :] = work((own_ref, qn_ref, qf_ref))

    @pl.when(part == 1)
    def _():
        work((own_ref, rn_ref, rf_ref))

    @pl.when(part == 2)
    def _():
        sums_ref[3:4, :] = work((own_ref, rn_ref, rf_ref))
        dh = dh_ref[...].T
        unit, inverse = normalise(x_ref[...].astype(F32))
        gain = full_row(at, mine_ref, theirs_ref, GAIN_ATTN)
        out_ref[...] = dx_ref[...] + normalise_back(dh, unit, inverse, gain)
        sums_ref[0:1, :] = jnp.sum(dh * unit, axis=0, keepdims=True)
        sums_ref[1:2, :] = jnp.sum(dh, axis=0, keepdims=True)


def back(place, dp, x, dx, mine, theirs, own, query_w, rest_w):
    rows, width = x.shape
    heads, parts, head, _ = dp.shape
    vectors = (x, dx, mine, theirs)
    return pl.pallas_call(
        back_body,
        grid_spec=pltpu.PrefetchScalarGridSpec(
            num_scalar_prefetch=1,
            grid=(parts,),
            in_specs=[pl.BlockSpec((heads, 1, head, rows), lambda t, _: (0, t, 0, 0))]
            + [whole(member.shape) for member in vectors]
            + [pl.BlockSpec((own.shape[0], width), lambda t, _: (0, t))]
            + [whole(member.shape) for member in query_w]
            + [pl.BlockSpec((member.shape[0], width), lambda t, _: (0, jnp.maximum(t - 1, 0))) for member in rest_w],
            out_specs=[whole((rows, width)), whole((8, width))],
            scratch_shapes=[pltpu.VMEM((width, rows), F32)],
        ),
        out_shape=[
            jax.ShapeDtypeStruct((rows, width), F32),
            jax.ShapeDtypeStruct((8, width), F32),
        ],
        compiler_params=params(),
        cost_estimate=about(8),
        name="back",
    )(place, dp, *vectors, own, *query_w, *rest_w)


def after(value, *others):
    return lax.optimization_barrier((value,) + others)[0]


def per_device(
    nctx, tokens_in, gain_attn, shift_attn, w_heads, bias_query, bias_value, w_merge, bias_merge, gain_mlp, shift_mlp,
    w_expand, bias_expand, w_contract, bias_contract, cotangent,
):
    seqs, tokens, width = tokens_in.shape
    rows = seqs * tokens
    half = width // 2
    heads = width // HEAD
    hidden = w_expand.shape[1]
    pairs = seqs * heads
    same = max(1, nctx // pairs)
    per = max(1, pairs // nctx)
    groups = seqs // per
    ctx = lax.axis_index("ctx")
    at = lax.axis_index("fsdp")
    core = ctx % 2
    place = jnp.stack([at, core]).astype(jnp.int32)

    def over_x(value):
        return lax.ppermute(value, "fsdp", [(0, 1), (1, 0)])

    def over_core(value):
        return lax.ppermute(value, "ctx", [(i, i ^ 1) for i in range(nctx)])

    def exchange(value):
        return lax.all_to_all(value, "ctx", 0, 0)

    def to_send(value):
        lead = value.shape[1:-1]
        value = value.reshape((heads,) + lead + (groups, per * tokens))
        value = jnp.moveaxis(value, -2, 1).reshape((nctx // same,) + lead + (per * tokens,))
        return value if same == 1 else jnp.repeat(value, same, axis=0)

    def received(value):
        value = value[::same]
        lead = value.shape[1:-1]
        value = value.reshape((heads, groups) + lead + (per * tokens,))
        return jnp.moveaxis(value, 1, -2).reshape((heads,) + lead + (rows,))

    def quarter_of(weight, first, count):
        size = weight.shape[0] // 2
        return lax.dynamic_slice(weight, (core * size, first), (size, count))

    def halves(value):
        mine = lax.dynamic_index_in_dim(value, at, 0, keepdims=False)
        return mine + over_x(lax.dynamic_index_in_dim(value, 1 - at, 0, keepdims=False))

    mine = jnp.concatenate(
        [
            member.reshape(-1, half)
            for member in (
                gain_attn, shift_attn, bias_query, bias_value, bias_merge, gain_mlp, shift_mlp, bias_contract,
                bias_expand, jnp.zeros(((-8 - bias_expand.shape[0] // half) % 16 * half,), BF16),
            )
        ]
    )
    theirs = over_x(mine)
    query_near = over_x(quarter_of(w_heads, 0, width))
    query_w = (query_near, over_core(query_near))
    shard = w_contract.shape[0] // nctx
    contract_shard = over_x(
        after(lax.dynamic_slice_in_dim(w_contract, ctx * shard, shard, 0), query_near)
    )
    contract_rest = lax.all_gather(contract_shard, "ctx", axis=0, tiled=False)
    rest_near = over_x(after(quarter_of(w_heads, width, 2 * width), query_near))
    rest_w = (rest_near, over_core(rest_near))
    expand_near = over_x(after(quarter_of(w_expand, 0, hidden), rest_near))
    merge_near = over_x(after(quarter_of(w_merge, 0, width), rest_near))

    x = tokens_in.reshape(rows, width)
    dy = cotangent.reshape(rows, width)
    dy_x = over_x(after(dy, expand_near))

    query_rows, normed = front_query(place, x, mine, theirs, w_heads, *query_w)
    query = exchange(to_send(query_rows))
    kv = exchange(to_send(front_rest(place, normed, mine, theirs, w_heads, *rest_w)))
    normed_all = lax.all_gather(after(normed, kv), "ctx", axis=0, tiled=False)
    mixed_b, mixed_f, lse = attend(query, kv, per)
    expand_w = (w_expand, expand_near, over_core(after(expand_near, lse)))
    merge_w = (w_merge, merge_near, over_core(after(merge_near, lse)))
    mixed = received(exchange(mixed_b)).reshape(width, rows)
    x1, normed_two, mixed_rows = merge(place, x, mixed, mine, theirs, merge_w)

    def of_four(value, there):
        return value, there, over_core(value), over_core(there)

    normed_four = of_four(normed_two, over_x(normed_two))
    dy_four = of_four(after(dy, lse), dy_x)
    mixed_x = over_x(mixed_rows)
    block_out, dx1, da, grad_mixed, sums_mlp, sums_expand = mlp(
        place, x1, normed_two, dy, mine, theirs, merge_w, expand_w, w_contract, contract_rest
    )
    grad_out = exchange(to_send(grad_mixed.reshape(heads, HEAD, rows)))

    grad_mlp = mlp_weights(
        place, nctx // 2, normed_four, dy_four, mine, theirs, expand_w, w_contract, contract_rest
    )
    chips = [[2 * chip + one for chip in range(nctx // 2)] for one in range(2)]
    grad_mlp = lax.psum_scatter(grad_mlp, "ctx", scatter_dimension=0, axis_index_groups=chips)
    grad_mlp = lax.all_gather(grad_mlp, "ctx", axis=0, tiled=False)
    contract_sum, expand_sum = spread_mlp(grad_mlp, w_contract.shape, w_expand.shape)

    grad_merge = merge_weights(place, (mixed_rows, mixed_x), (da, over_x(da)))
    vectors = halves(
        jnp.concatenate(
            [sums_mlp[:4].reshape(4, 2, half).swapaxes(0, 1), sums_expand.reshape(2, -1, half)], axis=1
        )
    )
    vectors = vectors.reshape(-1, width).astype(BF16)
    vectors = jnp.pad(vectors, ((0, -vectors.shape[0] % 16), (0, 0)))
    parcel = jnp.concatenate(
        [grad_merge.reshape(nctx, -1, width), jnp.broadcast_to(vectors, (nctx,) + vectors.shape)], axis=1
    )
    parcel = jnp.sum(exchange(parcel).astype(F32), axis=0)
    merge_part = parcel[: half // nctx].astype(BF16)
    vectors = parcel[half // nctx :].reshape(-1, half)

    dqkv = attend_back(query, kv, grad_out, mixed_f, lse, per)
    dp = received(exchange(dqkv))

    if groups > 1:
        normed_all = lax.dynamic_slice_in_dim(normed_all, (ctx // same % groups) * tokens * per, tokens * per, 1)
    grad_heads = heads_gradient(dqkv, normed_all)
    if groups > 1:
        members = [
            [first + one + same * group for group in range(groups)]
            for first in range(0, nctx, groups * same)
            for one in range(same)
        ]
        grad_heads = lax.psum(grad_heads, "ctx", axis_index_groups=members)
    kept = lax.dynamic_slice_in_dim(grad_heads, at * half, half, 1)
    sent = lax.dynamic_slice_in_dim(grad_heads, (1 - at) * half, half, 1)
    kept = (kept + over_x(sent.astype(BF16)).astype(F32)).astype(BF16)
    if groups * same > 1:
        share = kept.shape[0] // (groups * same)
        kept = lax.dynamic_slice_in_dim(kept, ctx % (groups * same) * share, share, 0)
    kept = jnp.concatenate([kept, merge_part[:, :half], merge_part[:, half:]])
    spread = lax.all_gather(kept, "ctx", axis=0, tiled=False)
    if groups * same > 1:
        share = 3 * HEAD // (groups * same)
        first = spread[:, :share].reshape(heads, 3 * HEAD, half)
        rest = spread[:, share:].reshape(heads, groups * same, 2, -1, half)
        rest = jnp.moveaxis(rest, 1, 2).reshape(heads, -1, half)
        spread = jnp.concatenate([first, rest], axis=1)
    heads_sum, merge_sum = spread_heads(spread, w_heads.shape, w_merge.shape)

    grad_tokens, sums_attn = back(place, dp, x, dx1, mine, theirs, w_heads, query_w, rest_w)
    last = halves(sums_attn[:4].reshape(4, 2, half).swapaxes(0, 1))
    last = jnp.sum(exchange(jnp.broadcast_to(last, (nctx,) + last.shape)), axis=0)
    return (
        block_out.reshape(tokens_in.shape),
        grad_tokens.reshape(tokens_in.shape),
        last[0],
        last[1],
        heads_sum,
        last[2],
        last[3],
        merge_sum,
        vectors[3],
        vectors[1],
        vectors[2],
        expand_sum,
        vectors[4 : 4 + hidden // width].reshape(-1),
        contract_sum,
        vectors[0],
    )


def solution(mesh):
    rows, vec, mat = P("fsdp", "ctx", None), P("fsdp"), P("fsdp", None)
    return jax.shard_map(
        functools.partial(per_device, mesh.shape["ctx"]),
        mesh=mesh,
        in_specs=(rows, vec, vec, mat, vec, vec, mat, vec, vec, vec, mat, vec, mat, vec, rows),
        out_specs=(rows, rows, vec, vec, mat, vec, vec, mat, vec, vec, vec, mat, vec, mat, vec),
        check_vma=False,
    )
```

time: 659 us -> 522 us (0.79)
  waiting for transfers between devices: 340 us -> 189 us
  local copies, waits for them, and re-layouts: 55.3 us -> 12.6 us
  blocking collectives: 60.2 us -> 102 us
  starting transfers between devices: 35.7 us -> 59.3 us
  other arithmetic: 16.3 us -> 3.76 us
    ppermute x13, waiting for transfers between devices: 243 us -> 84.8 us  [over_x(): return lax.ppermute(value, 'fsdp', [(0, 1), (1, 0)])]
    all_gather x4, waiting for transfers between devices: 0.03 us -> 48.1 us  [the longest x1 48 us: per_device(): grad_mlp = lax.all_gather(grad_mlp, 'ctx', axis=0, tiled=False)]
    all_to_all x2, blocking collectives: 60.2 us -> 102 us  [exchange(): return lax.all_to_all(value, 'ctx', 0, 0)]
    reduce_scatter x2 -> x1, waiting for transfers between devices: 40.2 us -> 3.28 us  [per_device(): lax.psum_scatter(grad_mlp, 'ctx', scatter_dimension=0, axis_index_groups=...]
    all_to_all x3 -> x5, starting transfers between devices: 15.9 us -> 38.2 us  [exchange(): return lax.all_to_all(value, 'ctx', 0, 0)]
    slice x7 -> x6, local copies, waits for them, and re-layouts: 18.9 us -> 1.21 us  [the longest x1 0.6 us: per_device(): last[3]]
    unnamed x59 -> x51, local copies, waits for them, and re-layouts: 20.7 us -> 3.79 us
    pallas_call x8 -> x10, Pallas kernels: 108 us -> 114 us  [the longest x1 24.8 us: mlp_weights(): pl.pallas_call(functools.partial(weights_body, own_steps), grid_spec=pltp...]
  transfers between devices with their start and end apart: 32 -> 31, of which waited for: 17 -> 18; matrix products, arithmetic and copies ran while one was open for 4% -> 2% of each run, Pallas kernels for 14% -> 24%
where the time goes in v2:
time: 522 us; the launch traced here: 514 us
  waiting for transfers between devices  189 us (36%)
  Pallas kernels  133 us (25%)
  blocking collectives  102 us (20%)
  starting transfers between devices  59.3 us (11%)
  between operations  14.8 us (3%)
  local copies, waits for them, and re-layouts  12.6 us (2%)
    all_to_all x2, blocking collectives, exchange(): return lax.all_to_all(value, 'ctx', 0, 0)  102 us
    ppermute x13, waiting for transfers between devices, over_x(): return lax.ppermute(value, 'fsdp', [(0, 1), (1, 0)])  84.8 us
    all_to_all x5, waiting for transfers between devices, exchange(): return lax.all_to_all(value, 'ctx', 0, 0)  51 us
    all_gather x1, waiting for transfers between devices, per_device(): grad_mlp = lax.all_gather(grad_mlp, 'ctx', axis=0, tiled=False)  48 us
    all_to_all x5, starting transfers between devices, exchange(): return lax.all_to_all(value, 'ctx', 0, 0)  38.2 us
    pallas_call x1, Pallas kernels, mlp_weights(): pl.pallas_call(functools.partial(weights_body, own_steps), grid_spec=pltp...  24.8 us
    pallas_call x1, Pallas kernels, mlp(): pl.pallas_call(functools.partial(mlp_body, own_steps), grid_spec=pltpu.Pr...  20.1 us
    pallas_call x1, Pallas kernels, attend_back(): pl.pallas_call(functools.partial(attend_back_body, per, tokens, block, ch...  19.7 us
  transfers between devices with their start and end apart: 31, of which 18 were waited for; matrix products, arithmetic and copies ran while one was open for 2% of the time, Pallas kernels for 24%

profile of v2, /device:TPU:0, one launch (start us, length us, event | category | flops | bytes accessed | tf_op | source)
XLA Modules:
  0.0 514.4 jit_solution(5263208487309216424)
XLA Ops:
  8.5 3.0 collective-permute-start.1
  12.5 11.0 %collective-permute-done.1.near.qn_ref = bf16[256,1024]{1,0:T(8,128)(2,1)S(1)} collective-permute-done((bf16[256,1024]{1,0:T(8,128)(2,1)S(1)}, bf16[256,1024]{1,0:T(8,128)(2,1)S(1)}, u32[]{:S(2)}, u32[]{:S(2)}) %collective-permute-start.1) | collective-permute-done | bytes 524320 | tf_op jit(solution)/shard_map/ppermute | solution.py:857
  23.5 1.7 collective-permute-start.9
  25.2 5.8 %collective-permute-done.9 = bf16[128,1024]{1,0:T(8,128)(2,1)S(1)} collective-permute-done((bf16[128,1024]{1,0:T(8,128)(2,1)S(1)}, bf16[128,1024]{1,0:T(8,128)(2,1)S(1)}, u32[]{:S(2)}, u32[]{:S(2)}) %collective-permute-start.9) | collective-permute-done | bytes 262176 | tf_op jit(solution)/shard_map/ppermute | solution.py:857
  33.0 1.5 collective-permute-start.3
  34.5 22.0 %collective-permute-done.3.rest_1_.rest_4_.rn_ref = bf16[256,2048]{1,0:T(8,128)(2,1)S(1)} collective-permute-done((bf16[256,2048]{1,0:T(8,128)(2,1)S(1)}, bf16[256,2048]{1,0:T(8,128)(2,1)S(1)}, u32[]{:S(2)}, u32[]{:S(2)}) %collective-permute-start.3) | collective-permute-done | bytes 1048608 | tf_op jit(solution)/shard_map/ppermute | solution.py:857
  58.5 2.6 collective-permute-done.theirs_ref.refs_9_
  61.9 5.1 front_query.1
  67.0 5.2 %front_rest.1 = bf16[16,2,64,256]{3,2,1,0:T(8,128)(2,1)S(1)} custom-call(s32[2]{0:T(128)S(1)} %pad_add_fusion.place, bf16[256,1024]{1,0:T(8,128)(2,1)} %get-tuple-element.62.h_ref, bf16[16,512]{1,0:T(8,128)(2,1)S(1)} %concatenate.12.mine_ref.refs_8_, bf16[16,512]{1,0:T(8,128)(2,1)S(1)} %collective-permute-done.theirs_ref.refs_9_, bf16[512,3072]{1,0:T(8,128)(2,1)} %own_ref.1, ...), custom_call_target="tpu_custom_call" | custom-call | flops 5750000128 | tf_op jit(solution)/shard_map/front_rest/pallas_call | solution.py:165
  72.2 30.6 %all_to_all.35.kv_ref = bf16[16,2,64,256]{3,2,1,0:T(8,128)(2,1)} all-to-all(bf16[16,2,64,256]{3,2,1,0:T(8,128)(2,1)S(1)} %front_rest.1), channel_id=1, replica_groups=mesh['ctx'=16,'fsdp'=2] {'ctx'}, dimensions={0} | all-to-all | bytes 2097152 | tf_op jit(solution)/shard_map/all_to_all | solution.py:863
  102.9 5.4 %all-to-all-start = ((bf16[16,64,256]{2,1,0:T(8,128)(2,1)}), bf16[16,64,256]{2,1,0:T(8,128)(2,1)S(1)}, u32[]{:S(2)}, u32[]{:S(2)}) async-start(bf16[16,64,256]{2,1,0:T(8,128)(2,1)} %get-tuple-element.44), calls=%async_computation | async-start | bytes 1048576 | tf_op jit(solution)/shard_map/all_to_all | solution.py:863
  108.4 3.1 constant_dynamic-slice_fusion.3
  111.6 1.4 collective-permute-start.5
  113.6 14.5 %all-to-all-done.query_ref = bf16[16,64,256]{2,1,0:T(8,128)(2,1)S(1)} async-done(((bf16[16,64,256]{2,1,0:T(8,128)(2,1)}), bf16[16,64,256]{2,1,0:T(8,128)(2,1)S(1)}, u32[]{:S(2)}, u32[]{:S(2)}) %all-to-all-start) | async-done | bytes 524320 | tf_op jit(solution)/shard_map/all_to_all | solution.py:863
  128.1 14.4 %attend.1 = (bf16[16,64,256]{2,1,0:T(8,128)(2,1)}, f32[16,64,256]{2,1,0:T(8,128)}, f32[4,8,512]{2,1,0:T(8,128)S(1)}) custom-call(bf16[16,64,256]{2,1,0:T(8,128)(2,1)S(1)} %all-to-all-done.query_ref, bf16[16,2,64,256]{3,2,1,0:T(8,128)(2,1)} %all_to_all.35.kv_ref), custom_call_target="tpu_custom_call" | custom-call | flops 23000000512 | tf_op jit(solution)/shard_map/attend/pallas_call | solution.py:258
  142.5 10.1 %all-to-all-start.2 = ((bf16[16,64,256]{2,1,0:T(8,128)(2,1)}), bf16[16,64,256]{2,1,0:T(8,128)(2,1)S(1)}, u32[]{:S(2)}, u32[]{:S(2)}) async-start(bf16[16,64,256]{2,1,0:T(8,128)(2,1)} %get-tuple-element.47), calls=%async_computation.2 | async-start | bytes 1048576 | tf_op jit(solution)/shard_map/all_to_all | solution.py:863
  153.1 17.8 %collective-permute-done.7.en_ref.refs_11_ = bf16[256,4096]{1,0:T(8,128)(2,1)} collective-permute-done((bf16[256,4096]{1,0:T(8,128)(2,1)}, bf16[256,4096]{1,0:T(8,128)(2,1)}, u32[]{:S(2)}, u32[]{:S(2)}) %collective-permute-start.7) | collective-permute-done | bytes 2097184 | tf_op jit(solution)/shard_map/ppermute | solution.py:857
  170.9 1.4 collective-permute-start.18
  172.3 3.2 all-to-all-done.2
  176.3 4.1 merge.1
  181.6 4.3 collective-permute-done.18.refs_5_
  186.4 10.2 %collective-permute-done.15.refs_1_ = bf16[256,1024]{1,0:T(8,128)(2,1)S(1)} collective-permute-done((bf16[256,1024]{1,0:T(8,128)(2,1)S(1)}, bf16[256,1024]{1,0:T(8,128)(2,1)S(1)}, u32[]{:S(2)}, u32[]{:S(2)}) %collective-permute-start.15) | collective-permute-done | bytes 524320 | tf_op jit(solution)/shard_map/ppermute | solution.py:857
  196.7 1.9 collective-permute-done.17.refs_3_
  199.4 24.8 %mlp_weights.1 = bf16[8,256,1024]{2,1,0:T(8,128)(2,1)} custom-call(s32[2]{0:T(128)S(1)} %pad_add_fusion.place, bf16[256,1024]{1,0:T(8,128)(2,1)S(1)} %get-tuple-element.52.h_ref.refs_0_, bf16[256,1024]{1,0:T(8,128)(2,1)S(1)} %collective-permute-done.15.refs_1_, bf16[256,1024]{1,0:T(8,128)(2,1)S(1)} %collective-permute-done.16.refs_2_, ...), custom_call_target="tpu_custom_call" | custom-call | flops 23000000512 | tf_op jit(solution)/shard_map/mlp_weights/pallas_call | solution.py:637
  224.2 1.6 collective-permute-start.12
  225.7 20.1 %mlp.1 = (bf16[256,1024]{1,0:T(8,128)(2,1)}, f32[256,1024]{1,0:T(8,128)}, bf16[256,1024]{1,0:T(8,128)(2,1)S(1)}, bf16[1024,256]{1,0:T(8,128)(2,1)}, f32[8,1024]{1,0:T(8,128)S(1)}, /*index=5*/f32[8,512]{1,0:T(8,128)S(1)}) custom-call(s32[2]{0:T(128)S(1)} %pad_add_fusion.place, f32[256,1024]{1,0:T(8,128)} %get-tuple-element.51.x1_ref, ...), custom_call_target="tpu_custom_call" | custom-call | flops 20700000256 | tf_op jit(solution)/shard_map/mlp/pallas_call | solution.py:516
  246.4 8.4 %all-to-all-start.3 = ((bf16[16,64,256]{2,1,0:T(8,128)(2,1)}), bf16[16,64,256]{2,1,0:T(8,128)(2,1)S(1)}, u32[]{:S(2)}, u32[]{:S(2)}) async-start(bf16[16,64,256]{2,1,0:T(8,128)(2,1)} %bitcast.7), calls=%async_computation.3 | async-start | bytes 1048576 | tf_op jit(solution)/shard_map/all_to_all | solution.py:863
  254.8 1.4 collective-permute-start.14
  256.2 3.7 collective-permute-done.14
  260.0 3.3 merge_weights.1
  263.3 2.6 pad_maximum_fusion
  265.9 11.9 %all-to-all-done.3.go_ref = bf16[16,64,256]{2,1,0:T(8,128)(2,1)S(1)} async-done(((bf16[16,64,256]{2,1,0:T(8,128)(2,1)}), bf16[16,64,256]{2,1,0:T(8,128)(2,1)S(1)}, u32[]{:S(2)}, u32[]{:S(2)}) %all-to-all-start.3) | async-done | bytes 524320 | tf_op jit(solution)/shard_map/all_to_all | solution.py:863
  277.8 7.5 %all-to-all-start.6 = ((bf16[16,48,1024]{2,1,0:T(8,128)(2,1)}), bf16[16,48,1024]{2,1,0:T(8,128)(2,1)S(1)}, u32[]{:S(2)}, u32[]{:S(2)}) async-start(bf16[16,48,1024]{2,1,0:T(8,128)(2,1)} %pad_maximum_fusion), calls=%async_computation.6 | async-start | bytes 3145728 | tf_op jit(solution)/shard_map/all_to_all | solution.py:863
  285.3 19.7 %attend_back.1.dp_ref = bf16[16,3,64,256]{3,2,1,0:T(8,128)(2,1)} custom-call(bf16[16,64,256]{2,1,0:T(8,128)(2,1)S(1)} %all-to-all-done.query_ref, bf16[16,2,64,256]{3,2,1,0:T(8,128)(2,1)} %all_to_all.35.kv_ref, bf16[16,64,256]{2,1,0:T(8,128)(2,1)S(1)} %all-to-all-done.3.go_ref, f32[16,64,256]{2,1,0:T(8,128)} %get-tuple-element.58.of_ref, ...), custom_call_target="tpu_custom_call" | custom-call | flops 28750000128 | tf_op jit(solution)/shard_map/attend_back/pallas_call | solution.py:352
  305.0 12.3 %all-to-all-done.6 = bf16[16,48,1024]{2,1,0:T(8,128)(2,1)S(1)} async-done(((bf16[16,48,1024]{2,1,0:T(8,128)(2,1)}), bf16[16,48,1024]{2,1,0:T(8,128)(2,1)S(1)}, u32[]{:S(2)}, u32[]{:S(2)}) %all-to-all-start.6) | async-done | bytes 1572896 | tf_op jit(solution)/shard_map/all_to_all | solution.py:863
  317.6 11.5 %heads_gradient.1 = f32[192,1024]{1,0:T(8,128)S(1)} custom-call(bf16[16,3,64,256]{3,2,1,0:T(8,128)(2,1)} %attend_back.1.dp_ref, bf16[16,256,1024]{2,1,0:T(8,128)(2,1)} %bitcast.59), custom_call_target="tpu_custom_call" | custom-call | flops 12650000384 | tf_op jit(solution)/shard_map/heads_gradient/pallas_call | solution.py:726
  329.2 1.7 collective-permute-start.11
  330.9 5.9 %collective-permute-done.11 = bf16[192,512]{1,0:T(8,128)(2,1)S(1)} collective-permute-done((bf16[192,512]{1,0:T(8,128)(2,1)S(1)}, bf16[192,512]{1,0:T(8,128)(2,1)S(1)}, u32[]{:S(2)}, u32[]{:S(2)}) %collective-permute-start.11) | collective-permute-done | bytes 196640 | tf_op jit(solution)/shard_map/ppermute | solution.py:857
  337.7 3.3 reduce-scatter.2.cloned.1.call-done
  341.0 71.3 %all_to_all.36.dp_ref = bf16[16,3,64,256]{3,2,1,0:T(8,128)(2,1)} all-to-all(bf16[16,3,64,256]{3,2,1,0:T(8,128)(2,1)S(1)} %copy-done.5), channel_id=1, replica_groups=mesh['ctx'=16,'fsdp'=2] {'ctx'}, dimensions={0} | all-to-all | bytes 3145728 | tf_op jit(solution)/shard_map/all_to_all | solution.py:863
  412.3 7.7 %back.1 = (f32[256,1024]{1,0:T(8,128)}, f32[8,1024]{1,0:T(8,128)S(1)}) custom-call(s32[2]{0:T(128)S(1)} %pad_add_fusion.place, bf16[16,3,64,256]{3,2,1,0:T(8,128)(2,1)} %all_to_all.36.dp_ref, bf16[256,1024]{1,0:T(8,128)(2,1)S(1)} %bitcast.44, f32[256,1024]{1,0:T(8,128)} %get-tuple-element.59.dx_ref, bf16[16,512]{1,0:T(8,128)(2,1)S(1)} %concatenate.12.mine_ref.refs_8_, ...), custom_call_target="tpu_custom_call" | custom-call | flops 9200000000 | tf_op jit(solution)/shard_map/back/pallas_call | solution.py:811
  420.1 2.2 collective-permute-start.10
  422.3 1.6 collective-permute-done.10
  424.6 6.9 %all-to-all-start.5 = ((f32[16,4,512]{2,1,0:T(4,128)}), f32[16,4,512]{2,1,0:T(4,128)S(1)}, u32[]{:S(2)}, u32[]{:S(2)}) async-start(f32[16,4,512]{2,1,0:T(4,128)} %broadcast_in_dim.6), calls=%async_computation.5 | async-start | bytes 262144 | tf_op jit(solution)/shard_map/all_to_all | solution.py:863
  432.7 9.1 %all-to-all-done.5 = f32[16,4,512]{2,1,0:T(4,128)S(1)} async-done(((f32[16,4,512]{2,1,0:T(4,128)}), f32[16,4,512]{2,1,0:T(4,128)S(1)}, u32[]{:S(2)}, u32[]{:S(2)}) %all-to-all-start.5) | async-done | bytes 131104 | tf_op jit(solution)/shard_map/all_to_all | solution.py:863
  442.5 6.7 %spread_heads.1 = (f32[512,3072]{1,0:T(8,128)}, f32[512,1024]{1,0:T(8,128)}) custom-call(bf16[16,256,512]{2,1,0:T(8,128)(2,1)} %bitcast.62), custom_call_target="tpu_custom_call" | custom-call | flops 10350000128 | tf_op jit(solution)/shard_map/spread_heads/pallas_call | solution.py:760
  449.1 48.0 %all-gather.8.cloned.1.call-done.in_ref = bf16[16,256,1024]{2,1,0:T(8,128)(2,1)} async-done(((bf16[1,256,1024]{2,1,0:T(8,128)(2,1)}), bf16[16,256,1024]{2,1,0:T(8,128)(2,1)}) %all-gather.8.cloned.1.call-update) | async-done | bytes 8388624 | tf_op jit(solution)/shard_map/all_gather | solution.py:937
  497.1 10.2 %spread_mlp.1 = (f32[2,8,128,1024]{3,2,1,0:T(8,128)}, f32[512,4096]{1,0:T(8,128)}) custom-call(bf16[16,256,1024]{2,1,0:T(8,128)(2,1)} %all-gather.8.cloned.1.call-done.in_ref), custom_call_target="tpu_custom_call" | custom-call | flops 9200000000 | tf_op jit(solution)/shard_map/spread_mlp/pallas_call | solution.py:673
  (125 shorter events, 15.9 us)
Async XLA Ops:
  7.2 49.9 %copy-start.10 = (bf16[512]{0:T(512)(128)(2,1)S(1)}, bf16[512]{0:T(512)(128)(2,1)}, u32[]{:S(2)}) copy-start(bf16[512]{0:T(512)(128)(2,1)} %param.16) | copy-start | bytes 3076
  7.2 49.8 %copy-start.11 = (bf16[512]{0:T(512)(128)(2,1)S(1)}, bf16[512]{0:T(512)(128)(2,1)}, u32[]{:S(2)}) copy-start(bf16[512]{0:T(512)(128)(2,1)} %param.17) | copy-start | bytes 3076
  7.2 49.9 %copy-start.12 = (bf16[512]{0:T(512)(128)(2,1)S(1)}, bf16[512]{0:T(512)(128)(2,1)}, u32[]{:S(2)}) copy-start(bf16[512]{0:T(512)(128)(2,1)} %param.19) | copy-start | bytes 3076
  7.2 49.9 %copy-start.13 = (bf16[512]{0:T(512)(128)(2,1)S(1)}, bf16[512]{0:T(512)(128)(2,1)}, u32[]{:S(2)}) copy-start(bf16[512]{0:T(512)(128)(2,1)} %param.20) | copy-start | bytes 3076
  7.2 49.9 %copy-start.14 = (bf16[512]{0:T(512)(128)(2,1)S(1)}, bf16[512]{0:T(512)(128)(2,1)}, u32[]{:S(2)}) copy-start(bf16[512]{0:T(512)(128)(2,1)} %param.22) | copy-start | bytes 3076
  7.2 49.9 %copy-start.15 = (bf16[512]{0:T(512)(128)(2,1)S(1)}, bf16[512]{0:T(512)(128)(2,1)}, u32[]{:S(2)}) copy-start(bf16[512]{0:T(512)(128)(2,1)} %param.23) | copy-start | bytes 3076
  7.2 49.9 %copy-start.16 = (bf16[512]{0:T(512)(128)(2,1)S(1)}, bf16[512]{0:T(512)(128)(2,1)}, u32[]{:S(2)}) copy-start(bf16[512]{0:T(512)(128)(2,1)} %param.24) | copy-start | bytes 3076
  7.3 49.9 %copy-start.17 = (bf16[512]{0:T(512)(128)(2,1)S(1)}, bf16[512]{0:T(512)(128)(2,1)}, u32[]{:S(2)}) copy-start(bf16[512]{0:T(512)(128)(2,1)} %param.28) | copy-start | bytes 3076
  7.3 49.9 %copy-start.9 = (bf16[2048]{0:T(1024)(128)(2,1)S(1)}, bf16[2048]{0:T(1024)(128)(2,1)}, u32[]{:S(2)}) copy-start(bf16[2048]{0:T(1024)(128)(2,1)} %param.26) | copy-start | bytes 12292
  7.3 54.6 %copy-start = (bf16[2,128,1024]{2,1,0:T(8,128)(2,1)S(1)}, bf16[2,128,1024]{2,1,0:T(8,128)(2,1)}, u32[]{:S(2)}) copy-start(bf16[2,128,1024]{2,1,0:T(8,128)(2,1)} %param.15) | copy-start | bytes 1572868
  7.3 192.1 %all-gather.10.cloned.1.call-start = ((), (), s32[]{:S(2)}) async-start(), calls=%async_computation.10 | async-start | bytes 4456448 | tf_op jit(solution)/shard_map/all_gather | solution.py:901
  8.5 14.9 %collective-permute-start.1 = (bf16[256,1024]{1,0:T(8,128)(2,1)S(1)}, bf16[256,1024]{1,0:T(8,128)(2,1)S(1)}, u32[]{:S(2)}, u32[]{:S(2)}) collective-permute-start(bf16[256,1024]{1,0:T(8,128)(2,1)S(1)} %constant_dynamic-slice_fusion.5), channel_id=1, source_target_pairs={{0,1},{1,0},{2,3},{3,2},{4,5},{5,4},{6,7},{7,6},{8,9},{9,8},{10,11... | collective-permute-start | bytes 1572872 | tf_op jit(solution)/shard_map/ppermute | solution.py:857
  23.5 37.6 %copy-start.1 = (bf16[256,1024]{1,0:T(8,128)(2,1)}, bf16[256,1024]{1,0:T(8,128)(2,1)S(1)}, u32[]{:S(2)}) copy-start(bf16[256,1024]{1,0:T(8,128)(2,1)S(1)} %collective-permute-done.1.near.qn_ref) | copy-start | bytes 1572868
  23.5 7.5 %collective-permute-start.9 = (bf16[128,1024]{1,0:T(8,128)(2,1)S(1)}, bf16[128,1024]{1,0:T(8,128)(2,1)S(1)}, u32[]{:S(2)}, u32[]{:S(2)}) collective-permute-start(bf16[128,1024]{1,0:T(8,128)(2,1)S(1)} %constant_dynamic-slice_fusion.2), channel_id=1, source_target_pairs={{0,1},{1,0},{2,3},{3,2},{4,5},{5,4},{6,7},{7,6},{8,9},{9,8},{10,11... | collective-permute-start | bytes 786440 | tf_op jit(solution)/shard_map/ppermute | solution.py:857
  31.7 285.9 %all-gather.12.cloned.1.call-start = ((), (), s32[]{:S(2)}) async-start(), calls=%async_computation.11 | async-start | bytes 8912896 | tf_op jit(solution)/shard_map/all_gather | solution.py:914
  33.0 23.5 %collective-permute-start.3 = (bf16[256,2048]{1,0:T(8,128)(2,1)S(1)}, bf16[256,2048]{1,0:T(8,128)(2,1)S(1)}, u32[]{:S(2)}, u32[]{:S(2)}) collective-permute-start(bf16[256,2048]{1,0:T(8,128)(2,1)S(1)} %constant_dynamic-slice_fusion.6), channel_id=1, source_target_pairs={{0,1},{1,0},{2,3},{3,2},{4,5},{5,4},{6,7},{7,6},{8,9},{9,8},{10,11... | collective-permute-start | bytes 3145736 | tf_op jit(solution)/shard_map/ppermute | solution.py:857
  56.5 10.5 %copy-start.18 = (bf16[256,2048]{1,0:T(8,128)(2,1)}, bf16[256,2048]{1,0:T(8,128)(2,1)S(1)}, u32[]{:S(2)}) copy-start(bf16[256,2048]{1,0:T(8,128)(2,1)S(1)} %collective-permute-done.3.rest_1_.rest_4_.rn_ref) | copy-start | bytes 3145732
  56.5 10.5 %collective-permute-start.4 = (bf16[256,2048]{1,0:T(8,128)(2,1)S(1)}, bf16[256,2048]{1,0:T(8,128)(2,1)}, u32[]{:S(2)}, u32[]{:S(2)}) collective-permute-start(bf16[256,2048]{1,0:T(8,128)(2,1)S(1)} %collective-permute-done.3.rest_1_.rest_4_.rn_ref), channel_id=1, source_target_pairs={{0,2},{2,0},{4,6},{6,4},{8,10},{10,8},{12,14},{14,12},{16,18},{18,... | collective-permute-start | bytes 3145736 | tf_op jit(solution)/shard_map/ppermute | solution.py:860
  56.5 4.6 collective-permute-start.2
  57.3 3.8 collective-permute-start
  72.2 36.1 %copy-start.8 = (bf16[512,1024]{1,0:T(8,128)(2,1)S(1)}, bf16[512,1024]{1,0:T(8,128)(2,1)}, u32[]{:S(2)}) copy-start(bf16[512,1024]{1,0:T(8,128)(2,1)} %mo_ref.3) | copy-start | bytes 3145732
  102.9 25.2 %all-to-all-start = ((bf16[16,64,256]{2,1,0:T(8,128)(2,1)}), bf16[16,64,256]{2,1,0:T(8,128)(2,1)S(1)}, u32[]{:S(2)}, u32[]{:S(2)}) async-start(bf16[16,64,256]{2,1,0:T(8,128)(2,1)} %get-tuple-element.44), calls=%async_computation | async-start | bytes 1048576 | tf_op jit(solution)/shard_map/all_to_all | solution.py:863
  111.6 41.0 %collective-permute-start.5 = (bf16[256,1024]{1,0:T(8,128)(2,1)S(1)}, bf16[256,1024]{1,0:T(8,128)(2,1)S(1)}, u32[]{:S(2)}, u32[]{:S(2)}) collective-permute-start(bf16[256,1024]{1,0:T(8,128)(2,1)S(1)} %constant_dynamic-slice_fusion.4), channel_id=1, source_target_pairs={{0,1},{1,0},{2,3},{3,2},{4,5},{5,4},{6,7},{7,6},{8,9},{9,8},{10,11... | collective-permute-start | bytes 1572872 | tf_op jit(solution)/shard_map/ppermute | solution.py:857
  113.0 57.9 %collective-permute-start.7 = (bf16[256,4096]{1,0:T(8,128)(2,1)}, bf16[256,4096]{1,0:T(8,128)(2,1)}, u32[]{:S(2)}, u32[]{:S(2)}) collective-permute-start(bf16[256,4096]{1,0:T(8,128)(2,1)} %constant_dynamic-slice_fusion.3), channel_id=1, source_target_pairs={{0,1},{1,0},{2,3},{3,2},{4,5},{5,4},{6,7},{7,6},{8,9},{9,8},{10,11... | collective-permute-start | bytes 6291464 | tf_op jit(solution)/shard_map/ppermute | solution.py:857
  142.5 33.1 %all-to-all-start.2 = ((bf16[16,64,256]{2,1,0:T(8,128)(2,1)}), bf16[16,64,256]{2,1,0:T(8,128)(2,1)S(1)}, u32[]{:S(2)}, u32[]{:S(2)}) async-start(bf16[16,64,256]{2,1,0:T(8,128)(2,1)} %get-tuple-element.47), calls=%async_computation.2 | async-start | bytes 1048576 | tf_op jit(solution)/shard_map/all_to_all | solution.py:863
  152.5 188.4 %reduce-scatter.2.cloned.1.call-start = ((), (), s32[]{:S(2)}) async-start(), calls=%async_computation.8 | async-start | bytes 4718592 | tf_op jit(solution)/shard_map/reduce_scatter | solution.py:936
  152.6 22.9 %copy-start.19 = (bf16[256,1024]{1,0:T(8,128)(2,1)}, bf16[256,1024]{1,0:T(8,128)(2,1)S(1)}, u32[]{:S(2)}) copy-start(bf16[256,1024]{1,0:T(8,128)(2,1)S(1)} %collective-permute-done.5.mn_ref) | copy-start | bytes 1572868
  152.6 19.7 %collective-permute-start.6 = (bf16[256,1024]{1,0:T(8,128)(2,1)S(1)}, bf16[256,1024]{1,0:T(8,128)(2,1)S(1)}, u32[]{:S(2)}, u32[]{:S(2)}) collective-permute-start(bf16[256,1024]{1,0:T(8,128)(2,1)S(1)} %collective-permute-done.5.mn_ref), channel_id=1, source_target_pairs={{0,2},{2,0},{4,6},{6,4},{8,10},{10,8},{12,14},{14,12},{16,18},{18,... | collective-permute-start | bytes 1572872 | tf_op jit(solution)/shard_map/ppermute | solution.py:860
  170.9 28.5 %collective-permute-start.8 = (bf16[256,4096]{1,0:T(8,128)(2,1)}, bf16[256,4096]{1,0:T(8,128)(2,1)}, u32[]{:S(2)}, u32[]{:S(2)}) collective-permute-start(bf16[256,4096]{1,0:T(8,128)(2,1)} %collective-permute-done.7.en_ref.refs_11_), channel_id=1, source_target_pairs={{0,2},{2,0},{4,6},{6,4},{8,10},{10,8},{12,14},{14,12},{16,18},{18,... | collective-permute-start | bytes 6291464 | tf_op jit(solution)/shard_map/ppermute | solution.py:860
  170.9 15.0 %collective-permute-start.18 = (bf16[256,1024]{1,0:T(8,128)(2,1)}, bf16[256,1024]{1,0:T(8,128)(2,1)}, u32[]{:S(2)}, u32[]{:S(2)}) collective-permute-start(bf16[256,1024]{1,0:T(8,128)(2,1)} %bitcast.4.dy_ref.refs_4_), channel_id=1, source_target_pairs={{0,1},{1,0},{2,3},{3,2},{4,5},{5,4},{6,7},{7,6},{8,9},{9,8},{10,11... | collective-permute-start | bytes 1572872 | tf_op jit(solution)/shard_map/ppermute | solution.py:857
  180.5 16.2 %collective-permute-start.15 = (bf16[256,1024]{1,0:T(8,128)(2,1)S(1)}, bf16[256,1024]{1,0:T(8,128)(2,1)S(1)}, u32[]{:S(2)}, u32[]{:S(2)}) collective-permute-start(bf16[256,1024]{1,0:T(8,128)(2,1)S(1)} %get-tuple-element.52.h_ref.refs_0_), channel_id=1, source_target_pairs={{0,1},{1,0},{2,3},{3,2},{4,5},{5,4},{6,7},{7,6},{8,9},{9,8},{10,11... | collective-permute-start | bytes 1572872 | tf_op jit(solution)/shard_map/ppermute | solution.py:857
  185.9 10.8 %collective-permute-start.20 = (bf16[256,1024]{1,0:T(8,128)(2,1)}, bf16[256,1024]{1,0:T(8,128)(2,1)S(1)}, u32[]{:S(2)}, u32[]{:S(2)}) collective-permute-start(bf16[256,1024]{1,0:T(8,128)(2,1)} %collective-permute-done.18.refs_5_), channel_id=1, source_target_pairs={{0,2},{2,0},{4,6},{6,4},{8,10},{10,8},{12,14},{14,12},{16,18},{18,... | collective-permute-start | bytes 1572872 | tf_op jit(solution)/shard_map/ppermute | solution.py:860
  185.9 10.8 %collective-permute-start.19 = (bf16[256,1024]{1,0:T(8,128)(2,1)}, bf16[256,1024]{1,0:T(8,128)(2,1)S(1)}, u32[]{:S(2)}, u32[]{:S(2)}) collective-permute-start(bf16[256,1024]{1,0:T(8,128)(2,1)} %bitcast.4.dy_ref.refs_4_), channel_id=1, source_target_pairs={{0,2},{2,0},{4,6},{6,4},{8,10},{10,8},{12,14},{14,12},{16,18},{18,... | collective-permute-start | bytes 1572872 | tf_op jit(solution)/shard_map/ppermute | solution.py:860
  186.4 10.3 %collective-permute-start.16 = (bf16[256,1024]{1,0:T(8,128)(2,1)S(1)}, bf16[256,1024]{1,0:T(8,128)(2,1)S(1)}, u32[]{:S(2)}, u32[]{:S(2)}) collective-permute-start(bf16[256,1024]{1,0:T(8,128)(2,1)S(1)} %get-tuple-element.52.h_ref.refs_0_), channel_id=1, source_target_pairs={{0,2},{2,0},{4,6},{6,4},{8,10},{10,8},{12,14},{14,12},{16,18},{18,... | collective-permute-start | bytes 1572872 | tf_op jit(solution)/shard_map/ppermute | solution.py:860
  196.6 1.9 collective-permute-start.17
  224.2 35.8 %collective-permute-start.12 = (bf16[256,1024]{1,0:T(8,128)(2,1)S(1)}, bf16[256,1024]{1,0:T(8,128)(2,1)S(1)}, u32[]{:S(2)}, u32[]{:S(2)}) collective-permute-start(bf16[256,1024]{1,0:T(8,128)(2,1)S(1)} %get-tuple-element.63.oo_ref), channel_id=1, source_target_pairs={{0,1},{1,0},{2,3},{3,2},{4,5},{5,4},{6,7},{7,6},{8,9},{9,8},{10,11... | collective-permute-start | bytes 1572872 | tf_op jit(solution)/shard_map/ppermute | solution.py:857
  245.8 14.1 %collective-permute-start.13 = (bf16[256,1024]{1,0:T(8,128)(2,1)S(1)}, bf16[256,1024]{1,0:T(8,128)(2,1)}, u32[]{:S(2)}, u32[]{:S(2)}) collective-permute-start(bf16[256,1024]{1,0:T(8,128)(2,1)S(1)} %get-tuple-element.64.ao_ref), channel_id=1, source_target_pairs={{0,1},{1,0},{2,3},{3,2},{4,5},{5,4},{6,7},{7,6},{8,9},{9,8},{10,11... | collective-permute-start | bytes 1572872 | tf_op jit(solution)/shard_map/ppermute | solution.py:857
  246.4 31.4 %all-to-all-start.3 = ((bf16[16,64,256]{2,1,0:T(8,128)(2,1)}), bf16[16,64,256]{2,1,0:T(8,128)(2,1)S(1)}, u32[]{:S(2)}, u32[]{:S(2)}) async-start(bf16[16,64,256]{2,1,0:T(8,128)(2,1)} %bitcast.7), calls=%async_computation.3 | async-start | bytes 1048576 | tf_op jit(solution)/shard_map/all_to_all | solution.py:863
  254.8 5.1 collective-permute-start.14
  277.8 39.5 %all-to-all-start.6 = ((bf16[16,48,1024]{2,1,0:T(8,128)(2,1)}), bf16[16,48,1024]{2,1,0:T(8,128)(2,1)S(1)}, u32[]{:S(2)}, u32[]{:S(2)}) async-start(bf16[16,48,1024]{2,1,0:T(8,128)(2,1)} %pad_maximum_fusion), calls=%async_computation.6 | async-start | bytes 3145728 | tf_op jit(solution)/shard_map/all_to_all | solution.py:863
  285.3 157.2 %all-gather.14.cloned.1.call-start = ((), (), s32[]{:S(2)}) async-start(), calls=%async_computation.12 | async-start | bytes 4456448 | tf_op jit(solution)/shard_map/all_gather | solution.py:975
  329.1 11.9 %copy-start.5 = (bf16[16,3,64,256]{3,2,1,0:T(8,128)(2,1)S(1)}, bf16[16,3,64,256]{3,2,1,0:T(8,128)(2,1)}, u32[]{:S(2)}) copy-start(bf16[16,3,64,256]{3,2,1,0:T(8,128)(2,1)} %attend_back.1.dp_ref) | copy-start | bytes 4718596
  329.1 83.2 %copy-start.2 = (bf16[256,1024]{1,0:T(8,128)(2,1)S(1)}, bf16[256,1024]{1,0:T(8,128)(2,1)}, u32[]{:S(2)}) copy-start(bf16[256,1024]{1,0:T(8,128)(2,1)} %copy-done.1) | copy-start | bytes 1572868
  329.1 83.2 %copy-start.4 = (bf16[256,1024]{1,0:T(8,128)(2,1)S(1)}, bf16[256,1024]{1,0:T(8,128)(2,1)}, u32[]{:S(2)}) copy-start(bf16[256,1024]{1,0:T(8,128)(2,1)} %copy-done.3) | copy-start | bytes 1572868
  329.2 7.6 %collective-permute-start.11 = (bf16[192,512]{1,0:T(8,128)(2,1)S(1)}, bf16[192,512]{1,0:T(8,128)(2,1)S(1)}, u32[]{:S(2)}, u32[]{:S(2)}) collective-permute-start(bf16[192,512]{1,0:T(8,128)(2,1)S(1)} %dynamic-slice_convert_fusion), channel_id=1, source_target_pairs={{0,1},{1,0},{2,3},{3,2},{4,5},{5,4},{6,7},{7,6},{8,9},{9,8},{10,11... | collective-permute-start | bytes 589832 | tf_op jit(solution)/shard_map/ppermute | solution.py:857
  337.6 159.5 %all-gather.8.cloned.1.call-start = ((), (), s32[]{:S(2)}) async-start(), calls=%async_computation.9 | async-start | bytes 8912896 | tf_op jit(solution)/shard_map/all_gather | solution.py:937
  420.1 3.8 collective-permute-start.10
  424.6 17.2 %all-to-all-start.5 = ((f32[16,4,512]{2,1,0:T(4,128)}), f32[16,4,512]{2,1,0:T(4,128)S(1)}, u32[]{:S(2)}, u32[]{:S(2)}) async-start(f32[16,4,512]{2,1,0:T(4,128)} %broadcast_in_dim.6), calls=%async_computation.5 | async-start | bytes 262144 | tf_op jit(solution)/shard_map/all_to_all | solution.py:863
  (7 other events, 10.1 us)
Sparse Core Ops, SparseCore 0:
  31.8 51.8 all-gather.9
  103.0 91.7 all-gather.11
  224.3 116.6 reduce-scatter.1
  343.8 74.0 all-gather.13
  420.1 76.9 all-gather.7
